TPU v7x, 32 devices: a whole 2x2x4 slice. The times are simulated.
32 devices in a mesh: dp: 16 (over z, y, x), head: 2 (over core).
Axes of the slice: x: 2, y: 2, z: 4, core: 2. Of those that a mesh axis runs over, the one named last changes fastest.
Arguments:
- tokens: bfloat16 [65536, 512], P(('dp', 'head')), may hold values from -6 to 6
- qkv_weight: bfloat16 [3, 512, 512], P(None, 'dp', 'head'), may hold values from -0.25 to 0.25
- out_weight: bfloat16 [512, 512], P('dp', 'head'), may hold values from -0.75 to 0.75
- up_weight: bfloat16 [512, 2048], P(('dp', 'head')), may hold values from -0.25 to 0.25
- down_weight: bfloat16 [2048, 512], P(('dp', 'head')), may hold values from -0.125 to 0.125
- norm_gains: bfloat16 [2, 512], P(None, ('dp', 'head')), may hold values from 0.099609375 to 1.8984375
- biases: bfloat16 [6, 512], P(None, ('dp', 'head')), may hold values from -3 to 3
- up_bias: bfloat16 [2048], P(('dp', 'head')), may hold values from -3 to 3
- segment: int32 [512, 128], P('dp'), may hold values from 0 to 15, as said below
- token_kinds: int32 [512, 128], P('dp'), may hold values from 0 to 2, as said below
- cotangent: bfloat16 [65536, 512], P(('dp', 'head')), may hold values from -6 to 6
Outputs:
- output: bfloat16 [65536, 512], P(('dp', 'head'))
- grad_tokens: float32 [65536, 512], P(('dp', 'head'))
- grad_qkv: float32 [3, 512, 512], P(None, 'dp', 'head')
- grad_out: float32 [512, 512], P('dp', 'head')
- grad_up: float32 [512, 2048], P(('dp', 'head'))
- grad_down: float32 [2048, 512], P(('dp', 'head'))
- grad_gains: float32 [2, 512], P(None, ('dp', 'head'))
- grad_biases: float32 [6, 512], P(None, ('dp', 'head'))
- grad_up_bias: float32 [2048], P(('dp', 'head'))
Inputs may be any that keep to these rules, and one draw needn't show every extreme that they name: `segment`: in each row the ids start at 0 and rise by one at the first token of each episode fragment; a fragment may be a single token; a row holds at most 16 fragments. `token_kinds`: within a fragment the kinds follow the cycle frame, action, delta, delta, delta, delta, starting at any place in that cycle.
All inputs are finite; a program needn't handle non-finite values.
Results may differ from a plain program's by a relative error of at most 0.014.
Values may be sent and summed in bfloat16 or wider, within the bound.
A program may use at most 192 MiB of HBM per device.

v0:
```python
import jax
import jax.numpy as jnp
from jax import lax
from jax.sharding import PartitionSpec as P

D = 512
HEAD_DIM = 64
SEQ = 128


eps_norm = 1e-05


def split_up(array, dim, count):
    before, after = (array.shape[:dim], array.shape[dim + 1 :])
    return jnp.moveaxis(array.reshape(*before, count, -1, *after), dim, 0)


def sent_and_summed(array, axis, dim):
    count = lax.axis_size(axis)
    pieces = lax.all_to_all(split_up(array, dim, count), axis, 0, 0, tiled=True)
    return jnp.sum(pieces.astype(jnp.float32), axis=0)


def layer_norm(values, gain, shift):
    center = values - jnp.mean(values, axis=-1, keepdims=True)
    variance = jnp.mean(center * center, axis=-1, keepdims=True)
    return center * lax.rsqrt(variance + eps_norm) * gain + shift


def gelu_exact(values):
    return jax.nn.gelu(values, approximate=False)


def visible(segment, token_kinds):
    is_delta = token_kinds == 2
    follows = (segment[:, 1:] == segment[:, :-1]) & is_delta[:, 1:] & is_delta[:, :-1]
    follows = jnp.concatenate([jnp.zeros_like(is_delta[:, :1]), follows], axis=1)
    run_id = jnp.cumsum(1 - follows.astype(jnp.int32), axis=1)
    position = lax.broadcasted_iota(jnp.int32, segment.shape, 1)
    same_seg = segment[:, :, None] == segment[:, None, :]
    causal = position[:, None, :] <= position[:, :, None]
    in_block = (run_id[:, :, None] == run_id[:, None, :]) & is_delta[:, :, None]
    return same_seg & (causal | in_block)


def attend_block(queries, keys_in, values_in, allowed, factor):
    scores = (
        jnp.einsum("rqhe,rkhe->rhqk", queries, keys_in, preferred_element_type=jnp.float32) * factor
    )
    scores = jnp.where(allowed[:, None], scores, -jnp.inf)
    row_max = jnp.max(scores, axis=-1, keepdims=True)
    exponent = jnp.exp(scores - row_max)
    row_sum = jnp.sum(exponent, axis=-1, keepdims=True)
    weights = (exponent / row_sum).astype(jnp.bfloat16)
    mixture = jnp.einsum("rhqk,rkhe->rqhe", weights, values_in, preferred_element_type=jnp.float32)
    log_total = row_max[..., 0] + jnp.log(row_sum[..., 0])
    return (mixture.astype(jnp.bfloat16), log_total)


def attend_back(queries, keys_in, values_in, allowed, log_total, grad_mix, factor):
    scores = (
        jnp.einsum("rqhe,rkhe->rhqk", queries, keys_in, preferred_element_type=jnp.float32) * factor
    )
    scores = jnp.where(allowed[:, None], scores, -jnp.inf)
    attention = jnp.exp(scores - log_total[..., None])
    grad_weight = jnp.einsum(
        "rqhe,rkhe->rhqk", grad_mix, values_in, preferred_element_type=jnp.float32
    )
    inner_sum = jnp.sum(attention * grad_weight, axis=-1, keepdims=True)
    grad_score = (attention * (grad_weight - inner_sum)).astype(jnp.bfloat16)
    grad_query = (
        jnp.einsum("rhqk,rkhe->rqhe", grad_score, keys_in, preferred_element_type=jnp.float32)
        * factor
    )
    grad_key = (
        jnp.einsum("rhqk,rqhe->rkhe", grad_score, queries, preferred_element_type=jnp.float32)
        * factor
    )
    grad_value = jnp.einsum(
        "rhqk,rqhe->rkhe",
        attention.astype(jnp.bfloat16),
        grad_mix,
        preferred_element_type=jnp.float32,
    )
    return jnp.stack([grad_query, grad_key, grad_value], axis=2).astype(jnp.bfloat16)


def on_device(
    tokens,
    qkv_weight,
    out_weight,
    up_weight,
    down_weight,
    norm_gains,
    biases,
    up_bias,
    segment,
    token_kinds,
    cotangent,
):
    head_index = lax.axis_index("head")
    qkv_local, out_local = (qkv_weight, out_weight)
    qkv_full, out_full = (
        lax.all_gather(qkv_local, "dp", axis=1, tiled=True),
        lax.all_gather(out_local, "dp", axis=0, tiled=True),
    )
    up_full, down_full, gain_full, bias_full, up_bias_full = (
        lax.all_gather(up_weight, ("dp", "head"), axis=0, tiled=True),
        lax.all_gather(down_weight, ("dp", "head"), axis=0, tiled=True),
        lax.all_gather(norm_gains, ("dp", "head"), axis=1, tiled=True),
        lax.all_gather(biases, ("dp", "head"), axis=1, tiled=True),
        lax.all_gather(up_bias, ("dp", "head"), axis=0, tiled=True),
    )
    gain_f32 = gain_full.astype(jnp.float32)
    bias_f32 = bias_full.astype(jnp.float32)
    width = qkv_full.shape[2]
    head_count = width // HEAD_DIM
    factor = HEAD_DIM ** (-0.5)
    column_start = head_index * width % D
    contract_last = (((1,), (1,)), ((), ()))
    contract_first = (((0,), (0,)), ((), ()))
    tokens_f32 = tokens.astype(jnp.float32)
    normed_f32, norm_one_back = jax.vjp(layer_norm, tokens_f32, gain_f32[0], bias_f32[0])
    normed = normed_f32.astype(jnp.bfloat16)
    group_normed = lax.all_gather(normed, "head", axis=0, tiled=True)
    group_tokens = group_normed.shape[0]
    row_count = group_tokens // SEQ
    block_rows = min(row_count, max(1, 512 // SEQ))
    block_count = row_count // block_rows
    query_bias = lax.dynamic_slice_in_dim(bias_f32[1], column_start, width)
    value_bias = lax.dynamic_slice_in_dim(bias_f32[2], column_start, width)
    bias_stack = jnp.stack([query_bias, jnp.zeros_like(query_bias), value_bias])
    projected = jnp.einsum(
        "td,sde->tse", group_normed, qkv_full, preferred_element_type=jnp.float32
    )
    packed = (projected + bias_stack).astype(jnp.bfloat16)
    allowed = visible(segment, token_kinds).reshape(block_count, block_rows, SEQ, SEQ)
    blocked = packed.reshape(block_count, block_rows, SEQ, 3, head_count, HEAD_DIM)

    def forward_block(inputs):
        block_in, mask_piece = inputs
        return attend_block(
            block_in[:, :, 0], block_in[:, :, 1], block_in[:, :, 2], mask_piece, factor
        )

    mixture, log_total = lax.map(forward_block, (blocked, allowed))
    mixture = mixture.reshape(group_tokens, width)
    rows_in = mixture
    branch = lax.psum_scatter(
        lax.dot_general(
            rows_in, out_full, contract_last, preferred_element_type=jnp.float32
        ).astype(jnp.bfloat16),
        "head",
        scatter_dimension=0,
        tiled=True,
    ).astype(jnp.float32)
    middle = tokens_f32 + (branch + bias_f32[3])
    normed_two_f32, norm_two_back = jax.vjp(layer_norm, middle, gain_f32[1], bias_f32[4])
    normed_two = normed_two_f32.astype(jnp.bfloat16)
    hidden_pre = jnp.dot(
        normed_two, up_full, preferred_element_type=jnp.float32
    ) + up_bias_full.astype(jnp.float32)
    hidden_f32, gelu_back = jax.vjp(gelu_exact, hidden_pre)
    hidden = hidden_f32.astype(jnp.bfloat16)
    output = middle + (jnp.dot(hidden, down_full, preferred_element_type=jnp.float32) + bias_f32[5])
    cotangent_f32 = cotangent.astype(jnp.float32)
    grad_down_part = lax.dot_general(
        hidden, cotangent, contract_first, preferred_element_type=jnp.float32
    )
    grad_bias_mlp = jnp.sum(cotangent_f32, axis=0)
    grad_hidden = lax.dot_general(
        cotangent, down_full, contract_last, preferred_element_type=jnp.float32
    )
    (grad_pre_f32,) = gelu_back(grad_hidden)
    grad_pre = grad_pre_f32.astype(jnp.bfloat16)
    grad_up_part = lax.dot_general(
        normed_two, grad_pre, contract_first, preferred_element_type=jnp.float32
    )
    grad_up_bias_part = jnp.sum(grad_pre.astype(jnp.float32), axis=0)
    grad_normed_two = lax.dot_general(
        grad_pre, up_full, contract_last, preferred_element_type=jnp.float32
    )
    grad_middle, grad_gain_two, grad_shift_two = norm_two_back(grad_normed_two)
    grad_middle = grad_middle + cotangent_f32
    grad_branch = grad_middle.astype(jnp.bfloat16)
    grad_bias_out = jnp.sum(grad_branch.astype(jnp.float32), axis=0)
    group_grad = lax.all_gather(grad_branch, "head", axis=0, tiled=True)
    grad_out_part = lax.dot_general(
        group_grad, mixture, contract_first, preferred_element_type=jnp.float32
    )
    grad_heads = jnp.dot(group_grad, out_full, preferred_element_type=jnp.float32).astype(
        jnp.bfloat16
    )
    grad_blocks = grad_heads.reshape(block_count, block_rows, SEQ, head_count, HEAD_DIM)

    def backward_block(inputs):
        block_in, mask_piece, log_piece, grad_piece = inputs
        return attend_back(
            block_in[:, :, 0],
            block_in[:, :, 1],
            block_in[:, :, 2],
            mask_piece,
            log_piece,
            grad_piece,
            factor,
        )

    grad_packed = lax.map(backward_block, (blocked, allowed, log_total, grad_blocks)).reshape(
        group_tokens, 3, width
    )
    grad_qkv_part = jnp.einsum(
        "td,tse->sde", group_normed, grad_packed, preferred_element_type=jnp.float32
    )
    bias_cols = jnp.sum(grad_packed.astype(jnp.float32), axis=0)
    zero_row = jnp.zeros((D,), jnp.float32)
    grad_query_bias = lax.dynamic_update_slice_in_dim(zero_row, bias_cols[0], column_start, 0)
    grad_value_bias = lax.dynamic_update_slice_in_dim(zero_row, bias_cols[2], column_start, 0)
    rows_in = grad_packed
    grad_normed = lax.psum_scatter(
        jnp.einsum("tse,sde->td", rows_in, qkv_full, preferred_element_type=jnp.float32).astype(
            jnp.bfloat16
        ),
        "head",
        scatter_dimension=0,
        tiled=True,
    ).astype(jnp.float32)
    grad_input, grad_gain_one, grad_shift_one = norm_one_back(grad_normed)
    grad_input = grad_input + grad_middle
    qkv_sum, out_sum = (
        sent_and_summed(grad_qkv_part.astype(jnp.bfloat16), "dp", 1),
        sent_and_summed(grad_out_part.astype(jnp.bfloat16), "dp", 0),
    )
    grad_gain_rows = jnp.stack([grad_gain_one, grad_gain_two])
    grad_bias_rows = jnp.stack(
        [
            grad_shift_one,
            grad_query_bias,
            grad_value_bias,
            grad_bias_out,
            grad_shift_two,
            grad_bias_mlp,
        ]
    )
    up_sum, down_sum, gain_sum, bias_sum, up_bias_sum = (
        lax.psum_scatter(grad_up_part, ("dp", "head"), scatter_dimension=0, tiled=True),
        lax.psum_scatter(grad_down_part, ("dp", "head"), scatter_dimension=0, tiled=True),
        lax.psum_scatter(grad_gain_rows, ("dp", "head"), scatter_dimension=1, tiled=True),
        lax.psum_scatter(grad_bias_rows, ("dp", "head"), scatter_dimension=1, tiled=True),
        lax.psum_scatter(grad_up_bias_part, ("dp", "head"), scatter_dimension=0, tiled=True),
    )
    return (
        output.astype(jnp.bfloat16),
        grad_input,
        qkv_sum,
        out_sum,
        up_sum,
        down_sum,
        gain_sum,
        bias_sum,
        up_bias_sum,
    )


def solution(mesh):
    in_specs = (
        P(("dp", "head"), None),
        P(None, "dp", "head"),
        P("dp", "head"),
        P(("dp", "head"), None),
        P(("dp", "head"), None),
        P(None, ("dp", "head")),
        P(None, ("dp", "head")),
        P(("dp", "head")),
        P("dp", None),
        P("dp", None),
        P(("dp", "head"), None),
    )
    out_specs = (
        P(("dp", "head"), None),
        P(("dp", "head"), None),
        P(None, "dp", "head"),
        P("dp", "head"),
        P(("dp", "head"), None),
        P(("dp", "head"), None),
        P(None, ("dp", "head")),
        P(None, ("dp", "head")),
        P(("dp", "head")),
    )
    return jax.shard_map(
        on_device, mesh=mesh, in_specs=in_specs, out_specs=out_specs, check_vma=False
    )
```

profile of v0, /device:TPU:0, one launch (start us, length us, event | category | flops | bytes accessed | tf_op | source)
XLA Modules:
  0.0 1115.6 jit_solution(7786211540712391827)
XLA Ops:
  8.1 43.8 %all-gather.1 = bf16[32,16,6]{1,2,0:T(8,128)(2,1)S(1)} all-gather(bf16[1,16,6]{1,2,0:T(8,128)(2,1)} %bitcast.213), channel_id=1, replica_groups=mesh['dp'=16,'head'=2] {'dp','head'}, dimensions={0}, use_global_device_ids=true | all-gather | bytes 6336 | tf_op jit(solution)/shard_map/all_gather | solution.py:112
  57.3 36.5 %all-gather = bf16[32,16,2]{1,2,0:T(2,128)(2,1)S(1)} all-gather(bf16[1,16,2]{1,2,0:T(2,128)(2,1)S(1)} %bitcast.218), channel_id=1, replica_groups=mesh['dp'=16,'head'=2] {'dp','head'}, dimensions={0}, use_global_device_ids=true | all-gather | bytes 2112 | tf_op jit(solution)/shard_map/all_gather | solution.py:111
  97.5 38.6 %all_gather.31 = bf16[512,256]{1,0:T(8,128)(2,1)S(1)} all-gather(bf16[32,256]{1,0:T(8,128)(2,1)S(1)} %copy-done.22), channel_id=1, replica_groups=mesh['dp'=16,'head'=2] {'dp'}, dimensions={0}, use_global_device_ids=true | all-gather | bytes 278528 | tf_op jit(solution)/shard_map/all_gather | solution.py:106
  137.6 43.0 %all_gather.30 = bf16[3,512,256]{2,1,0:T(8,128)(2,1)} all-gather(bf16[3,32,256]{2,1,0:T(8,128)(2,1)S(1)} %copy-done.21), channel_id=1, replica_groups=mesh['dp'=16,'head'=2] {'dp'}, dimensions={1}, use_global_device_ids=true | all-gather | bytes 835584 | tf_op jit(solution)/shard_map/all_gather | solution.py:105
  180.6 8.4 add_convert_fusion.1
  189.1 18.7 %reshape.238 = bf16[8,4,128,3,4,64]{5,4,2,1,0,3:T(4,128)(2,1)} reshape(bf16[4096,3,256]{2,0,1:T(8,128)(2,1)} %add_convert_fusion.1) | data formatting | bytes 12582912 | tf_op jit(solution)/shard_map/reshape | solution.py:139
  207.8 17.8 %copy.80 = bf16[8,4,128,3,4,64]{2,5,4,1,3,0:T(8,128)(2,1)} copy(bf16[8,4,128,3,4,64]{5,4,2,1,0,3:T(4,128)(2,1)} %reshape.238) | data formatting | bytes 12582912 | tf_op jit(solution)/shard_map/while | solution.py:147
  225.6 28.7 %while.22 = (s32[]{:T(128)}, bf16[8,4,128,4,64]{2,1,0,4,3:T(4,128)(2,1)}, f32[8,4,4,128]{3,2,1,0:T(4,128)}, bf16[8,4,128,3,4,64]{2,5,4,1,3,0:T(8,128)(2,1)}, pred[8,4,128,128]{2,3,1,0:T(8,128)(4,1)S(1)}, /*index=5*/s32[]{:T(128)}) while((s32[]{:T(128)}, bf16[8,4,128,4,64]{2,1,0,4,3:T(4,128)(2,1)}, f32[8,4,4,128]{3,2,1,0:T(4,128)}, ...), condition=%wide.region_6.7_spmd, body=%wide.region_3.6_spmd.sunk | while | flops 69335040 | bytes 6554701 | solution.py:147
  265.6 37.0 %all-reduce.1 = bf16[2048]{0:T(1024)(128)(2,1)S(1)} all-reduce(bf16[2048]{0:T(1024)(128)(2,1)S(1)} %dynamic-update-slice), channel_id=1, replica_groups=mesh['dp'=16,'head'=2] {'dp','head'}, use_global_device_ids=true, to_apply=%add.1 | all-reduce | flops 2048 | bytes 8192
  306.9 14.8 %all-gather.9.cloned.1.call-done = bf16[512,2048]{1,0:T(8,128)(2,1)} async-done(((bf16[16,2048]{1,0:T(8,128)(2,1)}), bf16[512,2048]{1,0:T(8,128)(2,1)}) %all-gather.9.cloned.1.call-update) | async-done | bytes 2097168 | tf_op jit(solution)/shard_map/all_gather | solution.py:109
  321.7 45.0 %multiply_convert_fusion.1 = (bf16[2048,2048]{1,0:T(8,128)(2,1)}, f32[2048,2048]{1,0:T(8,128)}, f32[2048,2048]{1,0:T(8,128)}) fusion(f32[2048]{0:T(1024)S(1)} %convert_element_type.111, bf16[512,2048]{1,0:T(8,128)(2,1)} %all-gather.9.cloned.1.call-done, f32[512]{0:T(512)S(1)} %bitcast.215, f32[512]{0:T(512)S(1)} %bitcast.204, f32[2048]{0:T(1024)S(1)} %fusion.54, ...), kind=kOutput, calls=%fused_computation.47 | convolution fusion | flops 4581228544 | bytes 48265216 | tf_op jit(solution)/shard_map/dot_general | solution.py:161
  366.7 13.6 %all-gather.11.cloned.1.call-done = bf16[2048,512]{1,0:T(8,128)(2,1)} async-done(((bf16[64,512]{1,0:T(8,128)(2,1)}), bf16[2048,512]{1,0:T(8,128)(2,1)}) %all-gather.11.cloned.1.call-update) | async-done | bytes 2097168 | tf_op jit(solution)/shard_map/all_gather | solution.py:110
  380.2 22.0 %convert_reduce_fusion = (f32[2048]{0:T(1024)S(1)}, bf16[2048,2048]{1,0:T(8,128)(2,1)}) fusion(f32[2048,2048]{1,0:T(8,128)} %get-tuple-element.150, bf16[2048,512]{1,0:T(8,128)(2,1)} %param.25, bf16[2048,512]{1,0:T(8,128)(2,1)} %all-gather.11.cloned.1.call-done, f32[2048,2048]{1,0:T(8,128)} %get-tuple-element.167, f32[2048]{0:T(1024)S(1)} %convert_element_type.111), kind=kOutput, calls=%fused_computation.45 | convolution fusion | flops 4366268416 | bytes 46153728 | tf_op jit(solution)/shard_map/dot_general | solution.py:172
  402.2 10.2 multiply_reduce_fusion.1
  417.8 12.6 %all-gather.13.cloned.1.call-done = bf16[4096,512]{1,0:T(8,128)(2,1)} async-done(((bf16[2048,512]{1,0:T(8,128)(2,1)}), bf16[4096,512]{1,0:T(8,128)(2,1)}) %all-gather.13.cloned.1.call-update) | async-done | bytes 4194320 | tf_op jit(solution)/shard_map/all_gather | solution.py:188
  435.2 7.2 reshape.233
  449.1 62.8 %while.23 = (s32[]{:T(128)}, bf16[8,4,128,3,4,64]{2,5,4,1,3,0:T(8,128)(2,1)}, bf16[8,4,128,3,4,64]{2,5,4,1,3,0:T(8,128)(2,1)}, pred[8,4,128,128]{2,3,1,0:T(8,128...) while((s32[]{:T(128)}, ...), condition=%wide.region_14.15_spmd, body=%wide.region_12.14_spmd.sunk | while | flops 173144064 | bytes 13870681 | solution.py:209
  511.9 10.3 copy.85
  522.2 11.2 %reshape.216 = bf16[4096,3,256]{0,2,1:T(8,128)(2,1)} reshape(bf16[8,4,128,3,4,64]{2,1,0,5,4,3:T(4,128)(2,1)} %copy.85) | data formatting | bytes 12582912 | tf_op jit(solution)/shard_map/reshape | solution.py:209
  533.4 7.9 bitcast_convert_fusion
  545.6 9.1 reduce-scatter.13.cloned.1.call-done
  561.5 7.1 convert_reduce_fusion.4
  569.6 11.0 fusion.55
  580.9 10.5 fusion.66
  591.4 40.7 %all-reduce.2 = f32[2048]{0:T(1024)S(1)} all-reduce(f32[2048]{0:T(1024)S(1)} %get-tuple-element.169), channel_id=8, replica_groups=mesh['dp'=16,'head'=2] {'dp','head'}, use_global_device_ids=true, to_apply=%region_32.33.clone | all-reduce | flops 2048 | bytes 16384
  643.1 8.3 fusion.48
  653.8 7.2 all-to-all-start
  661.0 11.0 add_convert_fusion.2
  680.4 16.8 %reduce-scatter.19.cloned.1.call-done = f32[16,2]{1,0:T(8,128)} async-done(((f32[512,2]{1,0:T(8,128)}), f32[16,2]{1,0:T(8,128)}) %reduce-scatter.19.cloned.1.call-update) | async-done | bytes 144
  698.5 130.3 %reduce-scatter.21.cloned.1.call-done = f32[16,6]{1,0:T(8,128)} async-done(((f32[512,6]{1,0:T(8,128)}), f32[16,6]{1,0:T(8,128)}) %reduce-scatter.21.cloned.1.call-update) | async-done | bytes 400
  830.1 138.3 %reduce-scatter.15.cloned.1.call-done = f32[16,2048]{1,0:T(8,128)} async-done(((f32[512,2048]{1,0:T(8,128)}), f32[16,2048]{1,0:T(8,128)}) %reduce-scatter.15.cloned.1.call-update) | async-done | bytes 131088 | tf_op jit(solution)/shard_map/reduce_scatter | solution.py:246
  968.4 139.6 %reduce-scatter.17.cloned.1.call-done = f32[64,512]{1,0:T(8,128)} async-done(((f32[2048,512]{1,0:T(8,128)}), f32[64,512]{1,0:T(8,128)}) %reduce-scatter.17.cloned.1.call-update) | async-done | bytes 131088 | tf_op jit(solution)/shard_map/reduce_scatter | solution.py:247
  (280 shorter events, 170.6 us)
Async XLA Ops:
  8.0 86.0 %copy-start = (bf16[2048,512]{1,0:T(8,128)(2,1)S(1)}, bf16[2048,512]{1,0:T(8,128)(2,1)}, u32[]{:S(2)}) copy-start(bf16[2048,512]{1,0:T(8,128)(2,1)} %param.15) | copy-start | bytes 6291460
  8.0 49.3 %copy-start.25 = (bf16[2,16]{1,0:T(2,128)(2,1)S(1)}, bf16[2,16]{1,0:T(2,128)(2,1)}, u32[]{:S(2)}) copy-start(bf16[2,16]{1,0:T(2,128)(2,1)} %param.20) | copy-start | bytes 196
  8.0 172.6 %all-gather.7.cloned.1.call-start = ((), (), s32[]{:S(2)}) async-start(), calls=%async_computation.8 | async-start | bytes 6291456 | tf_op jit(solution)/shard_map/all_gather | solution.py:126
  54.7 41.3 %copy-start.10 = (f32[2048]{0:T(1024)}, f32[2048]{0:T(1024)S(1)}, u32[]{:S(2)}) copy-start(f32[2048]{0:T(1024)S(1)} %broadcast_multiply_fusion.1) | copy-start | bytes 24580
  54.7 41.4 %copy-start.23 = (s32[32,128]{1,0:T(8,128)S(1)}, s32[32,128]{1,0:T(8,128)}, u32[]{:S(2)}) copy-start(s32[32,128]{1,0:T(8,128)} %param.24) | copy-start | bytes 49156
  54.7 41.4 %copy-start.12 = (s32[32,128]{1,0:T(8,128)S(1)}, s32[32,128]{1,0:T(8,128)}, u32[]{:S(2)}) copy-start(s32[32,128]{1,0:T(8,128)} %param.23) | copy-start | bytes 49156
  54.7 42.8 %copy-start.22 = (bf16[32,256]{1,0:T(8,128)(2,1)S(1)}, bf16[32,256]{1,0:T(8,128)(2,1)}, u32[]{:S(2)}) copy-start(bf16[32,256]{1,0:T(8,128)(2,1)} %param.17) | copy-start | bytes 49156
  57.3 36.5 %copy-start.15 = (f32[2048]{0:T(1024)}, f32[2048]{0:T(1024)S(1)}, u32[]{:S(2)}) copy-start(f32[2048]{0:T(1024)S(1)} %fusion.33) | copy-start | bytes 24580
  57.3 80.3 %copy-start.21 = (bf16[3,32,256]{2,1,0:T(8,128)(2,1)S(1)}, bf16[3,32,256]{2,1,0:T(8,128)(2,1)}, u32[]{:S(2)}) copy-start(bf16[3,32,256]{2,1,0:T(8,128)(2,1)} %param.16) | copy-start | bytes 147460
  57.3 78.9 %copy-start.13 = (f32[2048]{0:T(1024)}, f32[2048]{0:T(1024)S(1)}, u32[]{:S(2)}) copy-start(f32[2048]{0:T(1024)S(1)} %fusion.53) | copy-start | bytes 24580
  96.0 206.6 %reduce-scatter.11.cloned.1.call-start = ((), (), s32[]{:S(2)}) async-start(), calls=%async_computation.9 | async-start | bytes 6291456 | tf_op jit(solution)/shard_map/reduce_scatter | solution.py:150
  136.1 122.8 %copy-start.7 = (bf16[512,256]{1,0:T(8,128)(2,1)}, bf16[512,256]{1,0:T(8,128)(2,1)S(1)}, u32[]{:S(2)}) copy-start(bf16[512,256]{1,0:T(8,128)(2,1)S(1)} %all_gather.31) | copy-start | bytes 786436
  254.3 9.6 copy-start.6
  263.9 57.8 %all-gather.9.cloned.1.call-start = ((), (), s32[]{:S(2)}) async-start(), calls=%async_computation.10 | async-start | bytes 2162688 | tf_op jit(solution)/shard_map/all_gather | solution.py:109
  264.5 115.7 %all-gather.11.cloned.1.call-start = ((), (), s32[]{:S(2)}) async-start(), calls=%async_computation.11 | async-start | bytes 2162688 | tf_op jit(solution)/shard_map/all_gather | solution.py:110
  265.1 165.4 %all-gather.13.cloned.1.call-start = ((), (), s32[]{:S(2)}) async-start(), calls=%async_computation.12 | async-start | bytes 6291456 | tf_op jit(solution)/shard_map/all_gather | solution.py:188
  402.2 10.3 copy-start.18
  402.2 10.3 copy-start.3
  415.1 15.3 %copy-start.8 = (bf16[512,256]{1,0:T(8,128)(2,1)S(1)}, bf16[512,256]{1,0:T(8,128)(2,1)}, u32[]{:S(2)}) copy-start(bf16[512,256]{1,0:T(8,128)(2,1)} %copy-done.7) | copy-start | bytes 786436
  417.7 136.9 %reduce-scatter.13.cloned.1.call-start = ((), (), s32[]{:S(2)}) async-start(), calls=%async_computation.13 | async-start | bytes 6291456 | tf_op jit(solution)/shard_map/reduce_scatter | solution.py:220
  522.2 11.2 %copy-start.9 = (bf16[3,512,256]{2,1,0:T(8,128)(2,1)S(1)}, bf16[3,512,256]{2,1,0:T(8,128)(2,1)}, u32[]{:S(2)}) copy-start(bf16[3,512,256]{2,1,0:T(8,128)(2,1)} %all_gather.30) | copy-start | bytes 2359300
  541.3 13.4 %copy-start.11 = (f32[2048]{0:T(1024)S(1)}, f32[2048]{0:T(1024)}, u32[]{:S(2)}) copy-start(f32[2048]{0:T(1024)} %copy-done.10) | copy-start | bytes 24580
  541.3 13.4 %copy-start.20 = (f32[1,512]{1,0:T(1,128)S(1)}, f32[1,512]{1,0:T(1,128)}, u32[]{:S(2)}) copy-start(f32[1,512]{1,0:T(1,128)} %copy-done.19) | copy-start | bytes 6148
  541.3 16.8 %copy-start.16 = (f32[2048]{0:T(1024)S(1)}, f32[2048]{0:T(1024)}, u32[]{:S(2)}) copy-start(f32[2048]{0:T(1024)} %copy-done.15) | copy-start | bytes 24580
  541.3 16.8 %copy-start.14 = (f32[2048]{0:T(1024)S(1)}, f32[2048]{0:T(1024)}, u32[]{:S(2)}) copy-start(f32[2048]{0:T(1024)} %copy-done.13) | copy-start | bytes 24580
  541.3 155.8 %reduce-scatter.19.cloned.1.call-start = ((), (), s32[]{:S(2)}) async-start(), calls=%async_computation.16 | async-start | bytes 270336
  561.5 267.3 %reduce-scatter.21.cloned.1.call-start = ((), (), s32[]{:S(2)}) async-start(), calls=%async_computation.17 | async-start | bytes 270336
  569.5 398.9 %reduce-scatter.15.cloned.1.call-start = ((), (), s32[]{:S(2)}) async-start(), calls=%async_computation.14 | async-start | bytes 4325376 | tf_op jit(solution)/shard_map/reduce_scatter | solution.py:246
  580.6 527.4 %reduce-scatter.17.cloned.1.call-start = ((), (), s32[]{:S(2)}) async-start(), calls=%async_computation.15 | async-start | bytes 4325376 | tf_op jit(solution)/shard_map/reduce_scatter | solution.py:247
  637.6 16.2 %all-to-all-start.1 = ((bf16[16,32,256]{2,1,0:T(8,128)(2,1)}), bf16[16,32,256]{2,1,0:T(8,128)(2,1)S(1)}, u32[]{:S(2)}, u32[]{:S(2)}) async-start(bf16[16,32,256]{2,1,0:T(8,128)(2,1)} %bitcast.41), calls=%async_computation.3 | async-start | bytes 524288 | tf_op jit(solution)/shard_map/all_to_all | solution.py:21
  651.4 9.6 copy-start.24
  653.8 25.9 %all-to-all-start = ((bf16[16,3,32,256]{3,2,1,0:T(8,128)(2,1)}), bf16[16,3,32,256]{3,2,1,0:T(8,128)(2,1)S(1)}, u32[]{:S(2)}, u32[]{:S(2)}) async-start(bf16[16,3,32,256]{3,2,1,0:T(8,128)(2,1)} %copy.88), calls=%async_computation.2 | async-start | bytes 1572864 | tf_op jit(solution)/shard_map/all_to_all | solution.py:21
  (7 other events, 15.5 us)
Sparse Core Ops, SparseCore 0:
  96.1 11.1 all-gather.6
  264.0 9.5 reduce-scatter.10
  417.9 12.5 all-gather.12
  541.4 13.1 reduce-scatter.12
Sparse Core Ops, SparseCore 1:
  267.6 54.0 all-gather.8
  324.8 55.3 all-gather.10
  561.5 135.5 reduce-scatter.18
  699.5 129.2 reduce-scatter.20
  831.6 136.7 reduce-scatter.14
  971.3 136.7 reduce-scatter.16
where the time goes:
time: 1130 us; the launch traced here: 1120 us
  waiting for transfers between devices  483 us (43%)
  blocking collectives  240 us (21%)
  matrix products  186 us (16%)
  local copies, waits for them, and re-layouts  125 us (11%)
  other arithmetic  51.2 us (5%)
  between operations  16.3 us (1%)
  starting transfers between devices  13.8 us (1%)
    unnamed x12, waiting for transfers between devices  148 us
    reduce_scatter x1, waiting for transfers between devices, on_device(): lax.psum_scatter(grad_down_part, ('dp', 'head'), scatter_dimension=0, til...  140 us
    reduce_scatter x1, waiting for transfers between devices, on_device(): lax.psum_scatter(grad_up_part, ('dp', 'head'), scatter_dimension=0, tiled...  138 us
    unnamed x2, blocking collectives  77.8 us
    dot_general x1, matrix products, on_device(): jnp.dot(normed_two, up_full, preferred_element_type=jnp.float32)  45 us
    all_gather x1, blocking collectives, on_device(): lax.all_gather(biases, ('dp', 'head'), axis=1, tiled=True)  43.8 us
    all_gather x1, blocking collectives, on_device(): lax.all_gather(qkv_local, 'dp', axis=1, tiled=True)  43 us
    all_gather x1, blocking collectives, on_device(): lax.all_gather(out_local, 'dp', axis=0, tiled=True)  38.6 us
  transfers between devices with their start and end apart: 12, of which 9 were waited for; matrix products, arithmetic and copies ran while one was open for 10% of the time, Pallas kernels for 0%

commit v1 on v0

v1 whole, which is shorter than its diff:
```python
import math

import jax
import jax.numpy as jnp
from jax import lax
from jax.experimental import pallas as pl
from jax.experimental.pallas import tpu as pltpu
from jax.sharding import Mesh
from jax.sharding import PartitionSpec as P

bf16, f32 = jnp.bfloat16, jnp.float32
D = 512
SEQ = 128
LANES = 128
GRID_Z, GRID_P = 4, 4
EPS = 1e-5
MESH = pl.DeviceIdType.MESH
NN = (((1,), (0,)), ((), ()))
NT = (((1,), (1,)), ((), ()))
TN = (((0,), (0,)), ((), ()))
VMEM_LIMIT = (63 << 20) + (512 << 10)


def dot(a, b, dims=NN):
    return lax.dot_general(a, b, dims, preferred_element_type=f32)


def block(index, size):
    if isinstance(index, int):
        return pl.ds(index * size, size)
    return pl.ds(pl.multiple_of(index * size, size), size)


def parity(index):
    return index % 2 if isinstance(index, int) else lax.rem(index, 2)


class Place:
    def __init__(self):
        dp, self.h = lax.axis_index("dp"), lax.axis_index("head")
        self.z, self.p = dp // GRID_P, lax.rem(dp, GRID_P)
        x, y = lax.rem(self.p, 2), self.p // 2
        self.px = y * 2 + (1 - x)
        self.py = (1 - y) * 2 + x
        self.pd = (1 - y) * 2 + (1 - x)
        self.sib = 1 - self.h

    def at(self, z, p, h):
        return {"dp": z * GRID_P + p, "head": h}

    def line(self, k):
        return lax.rem(self.z + k, GRID_Z)

    def line_back(self, k):
        return lax.rem(self.z + (GRID_Z - k), GRID_Z)

    def plane(self):
        places = [(self.px, self.h), (self.py, self.h), (self.pd, self.h)]
        places += [(p, self.sib) for p in (self.p, self.px, self.py, self.pd)]
        return places


def barrier(me):
    sem = pltpu.get_barrier_semaphore()
    for p, h in me.plane():
        pl.semaphore_signal(sem, 1, device_id=me.at(me.z, p, h), device_id_type=MESH)
    for k in (1, 2, 3):
        pl.semaphore_signal(sem, 1, device_id=me.at(me.line(k), me.p, me.h), device_id_type=MESH)
    pl.semaphore_wait(sem, 10)


def remote(src, dst, send, recv, device):
    return pltpu.make_async_remote_copy(
        src_ref=src, dst_ref=dst, send_sem=send, recv_sem=recv, device_id=device, device_id_type=MESH
    )


class Gather:
    SENDS, RECVS = 11, 11

    def __init__(self, me, shard, view, send, recv, local):
        self.me, self.shard, self.view = me, shard, view
        self.send, self.recv, self.local = send, recv, local
        self.started = []

    def go(self, index, parts):
        def make():
            src, dst, device = parts()
            return remote(src, dst, self.send.at[index], self.recv.at[index], device)

        make().start()
        self.started.append(make)

    def landed(self, index, region):
        me = self.me
        remote(region, region, self.send.at[index], self.recv.at[index], me.at(me.z, me.p, me.sib)).wait_recv()

    def set_of(self, z, p):
        return self.view(z, p, self.me.h)

    def first(self):
        me = self.me
        self.mine = pltpu.make_async_copy(self.shard, self.set_of(me.z, me.p), self.local)
        self.mine.start()
        for k in (1, 2, 3):
            self.go(k - 1, lambda k=k: (self.shard, self.set_of(me.z, me.p), me.at(me.line(k), me.p, me.h)))

    def second(self):
        me = self.me
        self.mine.wait()
        for k in (1, 2, 3):
            self.landed(k - 1, self.view(me.line_back(k), me.p, me.h))
        line = lambda: self.set_of(pl.ds(0, 4), me.p)
        self.go(3, lambda: (line(), line(), me.at(me.z, me.px, me.h)))
        self.go(4, lambda: (line(), line(), me.at(me.z, me.py, me.h)))
        self.go(7, lambda: (line(), line(), me.at(me.z, me.p, me.sib)))

    def third(self):
        me = self.me
        from_x, from_y = lambda: self.set_of(pl.ds(0, 4), me.px), lambda: self.set_of(pl.ds(0, 4), me.py)
        half_x, half_y = lambda: self.set_of(pl.ds(0, 2), me.px), lambda: self.set_of(pl.ds(2, 2), me.py)
        self.landed(3, from_x())
        self.go(6, lambda: (half_x(), half_x(), me.at(me.z, me.py, me.h)))
        self.landed(4, from_y())
        self.go(5, lambda: (half_y(), half_y(), me.at(me.z, me.px, me.h)))
        self.go(8, lambda: (from_x(), from_x(), me.at(me.z, me.p, me.sib)))
        self.go(9, lambda: (from_y(), from_y(), me.at(me.z, me.p, me.sib)))

    def fourth(self):
        me = self.me
        self.landed(6, self.view(pl.ds(0, 2), me.pd, me.h))
        self.landed(5, self.view(pl.ds(2, 2), me.pd, me.h))
        diagonal = lambda: self.set_of(pl.ds(0, 4), me.pd)
        self.go(10, lambda: (diagonal(), diagonal(), me.at(me.z, me.p, me.sib)))

    def fifth(self):
        me = self.me
        for index, p in ((7, me.p), (8, me.px), (9, me.py), (10, me.pd)):
            self.landed(index, self.view(pl.ds(0, 4), p, me.sib))

    def close(self):
        for make in self.started:
            make().wait_send()


class SmallGather:
    SENDS, RECVS = 10, 10

    def __init__(self, me, tiles, send, recv):
        self.me, self.tiles, self.send, self.recv = me, tiles, send, recv
        self.started = []

    def go(self, index, parts):
        def make():
            region, device = parts()
            return remote(region, region, self.send.at[index], self.recv.at[index], device)

        make().start()
        self.started.append(make)

    def landed(self, index, region):
        me = self.me
        remote(region, region, self.send.at[index], self.recv.at[index], me.at(me.z, me.p, me.sib)).wait_recv()

    def first(self, gains, biases, up_bias):
        me = self.me
        place = lambda rows, width, start: dot(
            rows,
            jnp.where(
                lax.broadcasted_iota(jnp.int32, (width, LANES), 1)
                == lax.broadcasted_iota(jnp.int32, (width, LANES), 0) + start,
                1.0,
                0.0,
            ).astype(bf16),
        )
        start = (me.p * 2 + me.h) * 16
        rows = jnp.concatenate(
            [
                place(gains[...], 16, start),
                place(biases[...], 16, start),
                place(up_bias[...], 64, me.h * 64),
                jnp.zeros((7, LANES), f32),
            ],
            axis=0,
        )
        self.tiles[me.z, me.p, me.h] = rows.astype(bf16)

    def second(self):
        me = self.me
        for index, (p, h) in enumerate(me.plane()):
            self.go(index, lambda p=p, h=h: (self.tiles.at[me.z, me.p, me.h], me.at(me.z, p, h)))

    def third(self):
        me = self.me
        for index, (p, h) in enumerate(me.plane()):
            self.landed(index, self.tiles.at[me.z, p, h])
        for k in (1, 2, 3):
            self.go(6 + k, lambda k=k: (self.tiles.at[me.z], me.at(me.line(k), me.p, me.h)))

    def fourth(self, gain_bias, up_bias):
        me = self.me
        for k in (1, 2, 3):
            self.landed(6 + k, self.tiles.at[me.line_back(k)])
        for z in range(GRID_Z):
            total = jnp.zeros((8, LANES), f32)
            for p in range(GRID_P):
                pair = self.tiles[z, p, 0].astype(f32) + self.tiles[z, p, 1].astype(f32)
                total = total + pair[:8]
                up_bias[:, (z * GRID_P + p) * LANES : (z * GRID_P + p + 1) * LANES] = pair[8:9]
            gain_bias[:, z * LANES : (z + 1) * LANES] = total

    def close(self):
        for make in self.started:
            make().wait_send()


class Scatter:
    SENDS, RECVS = 8, 8

    def __init__(self, me, part, core, cross, sets, line, send, recv):
        self.me, self.part, self.core, self.cross, self.sets, self.line = me, part, core, cross, sets, line
        self.send, self.recv = send, recv
        self.started = []

    def go(self, index, parts):
        def make():
            src, dst, device = parts()
            return remote(src, dst, self.send.at[index], self.recv.at[index], device)

        make().start()
        self.started.append(make)

    def landed(self, index, region):
        me = self.me
        remote(region, region, self.send.at[index], self.recv.at[index], me.at(me.z, me.p, me.sib)).wait_recv()

    def first(self):
        me = self.me
        self.go(0, lambda: (self.part.at[me.sib], self.core, me.at(me.z, me.p, me.sib)))

    def second(self):
        me, part = self.me, self.part
        self.landed(0, self.core)

        def add(i, carry):
            z, p = i // GRID_P, lax.rem(i, GRID_P)
            part[me.h, z, p] = (part[me.h, z, p].astype(f32) + self.core[z, p].astype(f32)).astype(bf16)
            return carry

        lax.fori_loop(0, GRID_Z * GRID_P, add, 0)
        self.go(1, lambda: (part.at[me.h, pl.ds(0, 2), me.pd], self.cross.at[0], me.at(me.z, me.py, me.h)))
        self.go(2, lambda: (part.at[me.h, pl.ds(2, 2), me.pd], self.cross.at[1], me.at(me.z, me.px, me.h)))

    def third(self):
        me, part = self.me, self.part
        self.landed(1, self.cross.at[0])
        self.landed(2, self.cross.at[1])

        for i in range(2):
            part[me.h, i, me.px] = (part[me.h, i, me.px].astype(f32) + self.cross[0, i].astype(f32)).astype(bf16)
            part[me.h, 2 + i, me.py] = (
                part[me.h, 2 + i, me.py].astype(f32) + self.cross[1, i].astype(f32)
            ).astype(bf16)
        self.go(3, lambda: (part.at[me.h, :, me.px], self.sets.at[0], me.at(me.z, me.px, me.h)))
        self.go(4, lambda: (part.at[me.h, :, me.py], self.sets.at[1], me.at(me.z, me.py, me.h)))

    def fourth(self):
        me, part = self.me, self.part
        self.landed(3, self.sets.at[0])
        self.landed(4, self.sets.at[1])
        for i in range(GRID_Z):
            part[me.h, i, me.p] = (
                part[me.h, i, me.p].astype(f32) + self.sets[0, i].astype(f32) + self.sets[1, i].astype(f32)
            ).astype(bf16)
        for k in (1, 2, 3):
            self.go(
                4 + k,
                lambda k=k: (
                    part.at[me.h, me.line(k), me.p], self.line.at[k - 1], me.at(me.line(k), me.p, me.h)
                ),
            )

    def fifth(self):
        me = self.me
        total = self.part[me.h, me.z, me.p].astype(f32)
        for k in (1, 2, 3):
            self.landed(4 + k, self.line.at[k - 1])
            total = total + self.line[k - 1].astype(f32)
        return total

    def close(self):
        for make in self.started:
            make().wait_send()


class SmallScatter:
    SENDS, RECVS = 10, 10

    def __init__(self, me, part, line, sets, send, recv):
        self.me, self.part, self.line, self.sets = me, part, line, sets
        self.send, self.recv = send, recv
        self.started = []

    def go(self, index, parts):
        def make():
            src, dst, device = parts()
            return remote(src, dst, self.send.at[index], self.recv.at[index], device)

        make().start()
        self.started.append(make)

    def landed(self, index, region):
        me = self.me
        remote(region, region, self.send.at[index], self.recv.at[index], me.at(me.z, me.p, me.sib)).wait_recv()

    def first(self):
        me = self.me
        for k in (1, 2, 3):
            self.go(
                k - 1,
                lambda k=k: (self.part.at[me.line(k)], self.line.at[k - 1], me.at(me.line(k), me.p, me.h)),
            )

    def second(self):
        me = self.me
        total = self.part[me.z]
        for k in (1, 2, 3):
            self.landed(k - 1, self.line.at[k - 1])
            total = total + self.line[k - 1]
        self.sets[7] = total
        for index, (p, h) in enumerate(me.plane()):
            self.go(
                3 + index, lambda i=index, p=p, h=h: (self.sets.at[7], self.sets.at[i], me.at(me.z, p, h))
            )

    def third(self, gains, biases, up_bias):
        me = self.me
        total = self.sets[7]
        for index in range(7):
            self.landed(3 + index, self.sets.at[index])
            total = total + self.sets[index]
        rows = pltpu.roll(total[:8], LANES - 16 * (me.p * 2 + me.h), 1)
        gains[...] = rows[0:2, 0:16]
        biases[...] = rows[2:8, 0:16]
        row = lax.broadcasted_iota(jnp.int32, (8, LANES), 0)
        hidden = jnp.sum(jnp.where(row == me.p, total[8:], 0.0), axis=0, keepdims=True)
        hidden = jnp.where(me.h == 0, hidden[:, 0:64], hidden[:, 64:128])
        up_bias[...] = hidden

    def close(self):
        for make in self.started:
            make().wait_send()


ANY = pl.BlockSpec(memory_space=pl.ANY)
VM = pl.BlockSpec(memory_space=pltpu.VMEM)


def normalized(x):
    center = x - jnp.mean(x, axis=-1, keepdims=True)
    rstd = lax.rsqrt(jnp.mean(center * center, axis=-1, keepdims=True) + EPS)
    return center * rstd, rstd


def norm_back(e, xhat, rstd, gain):
    u = e * gain
    return rstd * (
        u - jnp.mean(u, axis=-1, keepdims=True) - xhat * jnp.mean(u * xhat, axis=-1, keepdims=True)
    )


def column_sums(x):
    return jnp.sum(x.reshape(x.shape[0] // 8, 8, x.shape[1]), axis=0)


def gelu_and_slope(u):
    phi = 0.5 + 0.5 * lax.erf(u * math.sqrt(0.5))
    return u * phi, phi + u * (jnp.exp(u * u * -0.5) * (1 / math.sqrt(2 * math.pi)))


def two_heads(x):
    first = lax.broadcasted_iota(jnp.int32, x.shape, 1) < 64
    zero = jnp.zeros_like(x)
    return jnp.concatenate([jnp.where(first, x, zero), jnp.where(first, zero, x)], axis=0)


def tiles(ref, rows):
    return jnp.concatenate([ref[p, rows] for p in range(4)], axis=1)


def hidden_masks(segment, kinds, mask):
    s, k = segment, kinds
    position = lax.broadcasted_iota(jnp.int32, s.shape, 1)
    follows = (s == pltpu.roll(s, 1, 1)) & (k == 2) & (pltpu.roll(k, 1, 1) == 2) & (position > 0)
    upper = lax.broadcasted_iota(jnp.int32, (SEQ, SEQ), 0) <= lax.broadcasted_iota(jnp.int32, (SEQ, SEQ), 1)
    run = dot(jnp.where(follows, 0.0, 1.0).astype(bf16), jnp.where(upper, 1.0, 0.0).astype(bf16))
    seg = s.astype(f32)
    for r in range(s.shape[0]):
        seg_j = jnp.broadcast_to(seg[r : r + 1], (SEQ, SEQ))
        run_j = jnp.broadcast_to(run[r : r + 1], (SEQ, SEQ))
        mask[r] = jnp.where((seg_j.T == seg_j) & (run_j <= run_j.T), 0.0, -jnp.inf).astype(bf16)


def layer_kernel(
    tokens_hbm, cot_hbm, qkv_s, out_s, up_s, down_s, gains, biases, up_bias, segment, kinds,
    output_hbm, grad_hbm, g_qkv, g_out, g_up, g_down, g_gains, g_biases, g_up_bias,
    tok, cot, w_qkv, w_out, w_up, w_down, gb, upb, mask,
    normed, packed, att, mix, hid, gpre, gbr, gmix, acc, acc_up, acc_q,
    out_stage, grad_stage,
    p_down, p_up, p_out, p_qkv, p_small,
    core0, core1, core2, core3, cross0, cross1, cross2, cross3,
    sets0, sets1, sets2, sets3, line0, line1, line2, line3,
    small_tiles, small_line, small_sets,
    g_send, g_recv, g_local, s_send, s_recv, io_sem, out_sem,
):
    T = tok.shape[0]
    ROWS = T // SEQ
    me = Place()
    load_tok = pltpu.make_async_copy(tokens_hbm, tok, io_sem.at[0])
    load_cot = pltpu.make_async_copy(cot_hbm, cot, io_sem.at[1])
    load_tok.start()
    load_cot.start()

    def qkv_view(s):
        return lambda z, p, h: w_qkv.at[s, z, p, :, pl.ds(pl.multiple_of(h * 256, 256), 256)]

    views = [(qkv_s.at[s], qkv_view(s)) for s in range(3)]
    views += [
        (out_s, lambda z, p, h: w_out.at[z, p, :, pl.ds(pl.multiple_of(h * 256, 256), 256)]),
        (up_s, lambda z, p, h: w_up.at[z, p, h]),
        (down_s, lambda z, p, h: w_down.at[z, p, h]),
    ]
    big = [
        Gather(me, shard, view, g_send.at[i], g_recv.at[i], g_local.at[i])
        for i, (shard, view) in enumerate(views)
    ]
    attn_w, mlp_w = big[:3], big[3:]
    small = SmallGather(me, small_tiles, g_send.at[6], g_recv.at[6])
    small.first(gains, biases, up_bias)
    barrier(me)
    small.second()
    for g in attn_w:
        g.first()
    own_rows = pl.ds(pl.multiple_of(me.h * ROWS, ROWS), ROWS)
    hidden_masks(segment[own_rows, :], kinds[own_rows, :], mask)
    small.third()
    for g in attn_w:
        g.second()
    small.fourth(gb, upb)
    load_tok.wait()

    def norm_one(i, carry):
        r = block(i, 256)
        xhat, _ = normalized(tok[r, :].astype(f32))
        normed[r, :] = (xhat * gb[0:1, :] + gb[2:3, :]).astype(bf16)
        return carry

    lax.fori_loop(0, T // 256, norm_one, 0)
    for g in attn_w:
        g.third()
    for g in mlp_w:
        g.first()
    for g in attn_w:
        g.fourth()
    for g in attn_w:
        g.fifth()

    def project(i, carry):
        r = block(i, 512)
        x = normed[r, :]
        q = (dot(x, w_qkv[0].reshape(D, D)) + gb[3:4, :]).astype(bf16) * jnp.asarray(0.125, bf16)
        k = dot(x, w_qkv[1].reshape(D, D)).astype(bf16)
        v = (dot(x, w_qkv[2].reshape(D, D)) + gb[4:5, :]).astype(bf16)
        for p in range(4):
            for s, value in enumerate((q, k, v)):
                packed[s, p, r, :] = value[:, LANES * p : LANES * p + LANES]
        return carry

    lax.fori_loop(0, T // 512, project, 0)
    for g in mlp_w:
        g.second()

    def attend(i, carry):
        for r in (2 * i, 2 * i + 1):
            rows = block(r, SEQ)
            hide = mask[r].astype(f32)
            for p in range(4):
                keys, values = two_heads(packed[1, p, rows, :]), two_heads(packed[2, p, rows, :])
                scores = dot(packed[0, p, rows, :], keys, NT)
                weights = []
                for h in range(2):
                    t = scores[:, SEQ * h : SEQ * h + SEQ] + hide
                    e = jnp.exp(t - jnp.max(t, axis=-1, keepdims=True))
                    a = (e * (1.0 / jnp.sum(e, axis=-1, keepdims=True))).astype(bf16)
                    att[r, 2 * p + h] = a
                    weights.append(a)
                mix[p, rows, :] = dot(jnp.concatenate(weights, axis=1), values).astype(bf16)

        @pl.when(i == 3)
        def _():
            for g in mlp_w:
                g.third()

        @pl.when(i == 6)
        def _():
            for g in mlp_w:
                g.fourth()

        return carry

    lax.fori_loop(0, ROWS // 2, attend, 0)
    load_cot.wait()
    for g in mlp_w:
        g.fifth()

    acc[...] = jnp.zeros_like(acc)
    acc_up[...] = jnp.zeros_like(acc_up)
    BM = out_stage.shape[1]

    def out_copy(i):
        return pltpu.make_async_copy(
            out_stage.at[parity(i)], output_hbm.at[block(i, BM), :], out_sem.at[parity(i)]
        )

    def feed_forward(i, carry):
        r = block(i, BM)

        @pl.when(i >= 2)
        def _():
            out_copy(i - 2).wait()

        middle = tok[r, :].astype(f32) + dot(tiles(mix, r), w_out[...].reshape(D, D), NT) + gb[5:6, :]
        xhat, rstd = normalized(middle)
        two = (xhat * gb[1:2, :] + gb[6:7, :]).astype(bf16)
        tok[r, :] = two
        c = cot[r, :]
        total = middle + gb[7:8, :]
        e = jnp.zeros((BM, D), f32)
        for j in range(4):
            cols = slice(512 * j, 512 * j + 512)
            w_up_j = w_up[:, :, :, :, cols].reshape(D, 512)
            w_down_j = w_down[j].reshape(512, D)
            u = dot(two, w_up_j) + upb[:, cols]
            grad_hidden = dot(c, w_down_j, NT)
            hidden, slope = gelu_and_slope(u)
            hidden = hidden.astype(bf16)
            hid[r, cols] = hidden
            total = total + dot(hidden, w_down_j)
            grad_pre = grad_hidden * slope
            acc_up[:, cols] += column_sums(grad_pre)
            grad_pre = grad_pre.astype(bf16)
            gpre[r, cols] = grad_pre
            e = e + dot(grad_pre, w_up_j, NT)
        out_stage[parity(i)] = total.astype(bf16)
        out_copy(i).start()
        cot_f32 = c.astype(f32)
        branch = (cot_f32 + norm_back(e, xhat, rstd, gb[1:2, :])).astype(bf16)
        gbr[r, :] = branch
        grad_mix = dot(branch, w_out[...].reshape(D, D)).astype(bf16)
        for p in range(4):
            gmix[p, r, :] = grad_mix[:, LANES * p : LANES * p + LANES]
        acc[1] += column_sums(e * xhat)
        acc[6] += column_sums(e)
        acc[5] += column_sums(branch.astype(f32))
        acc[7] += column_sums(cot_f32)
        return carry

    count = T // BM
    lax.fori_loop(0, count, feed_forward, 0)

    units = [
        Scatter(me, *refs, s_send.at[i], s_recv.at[i])
        for i, refs in enumerate(
            (
                (p_down, core0, cross0, sets0, line0),
                (p_up, core1, cross1, sets1, line1),
                (p_out, core2, cross2, sets2, line2),
                (p_qkv, core3, cross3, sets3, line3),
            )
        )
    ]
    down_u, up_u, out_u, qkv_u = units

    def grad_down_chunk(z, carry):
        o = dot(hid[:, block(z, 512)], cot[...], TN).astype(bf16)
        for p in range(GRID_P):
            for h in range(2):
                for j in range(4):
                    p_down[h, z, p, 64 * j : 64 * j + 64] = o[
                        64 * (2 * p + h) : 64 * (2 * p + h) + 64, LANES * j : LANES * j + LANES
                    ]
        return carry

    lax.fori_loop(0, 4, grad_down_chunk, 0)
    down_u.first()

    def grad_up_chunk(c, carry):
        o = dot(tok[...], gpre[:, block(c, 512)], TN).astype(bf16)
        for z in range(GRID_Z):
            for p in range(GRID_P):
                for h in range(2):
                    d = (z * 4 + p) * 2 + h
                    for j in range(4):
                        p_up[h, z, p, pl.ds(pl.multiple_of(64 * c + 16 * j, 16), 16)] = o[
                            16 * d : 16 * d + 16, LANES * j : LANES * j + LANES
                        ]
        return carry

    lax.fori_loop(0, 4, grad_up_chunk, 0)
    up_u.first()
    load_tok = pltpu.make_async_copy(tokens_hbm, tok, io_sem.at[0])
    load_tok.start()
    down_u.second()

    o = dot(gbr[...], jnp.concatenate([mix[p] for p in range(4)], axis=1), TN).astype(bf16)
    for z in range(GRID_Z):
        for p in range(GRID_P):
            d = z * 4 + p
            for h in range(2):
                for j in range(2):
                    p_out[h, z, p, 32 * j : 32 * j + 32] = o[
                        32 * d : 32 * d + 32, 256 * h + LANES * j : 256 * h + LANES * j + LANES
                    ]
    out_u.first()

    def attend_back(half):
        def body(r, carry):
            rows = block(r, SEQ)
            for pp in range(2):
                p = 2 * half + pp
                queries, keys = two_heads(packed[0, p, rows, :]), two_heads(packed[1, p, rows, :])
                values = two_heads(packed[2, p, rows, :])
                grad = gmix[p, rows, :]
                grad_two = two_heads(grad)
                grad_weight = dot(grad, values, NT)
                product = grad.astype(f32) * mix[p, rows, :].astype(f32)
                first = lax.broadcasted_iota(jnp.int32, (SEQ, LANES), 1) < 64
                scores, weights = [], []
                for h in range(2):
                    inner = jnp.sum(jnp.where(first == (h == 0), product, 0.0), axis=-1, keepdims=True)
                    a = att[r, 2 * p + h]
                    weights.append(a)
                    scores.append(
                        (a.astype(f32) * (grad_weight[:, SEQ * h : SEQ * h + SEQ] - inner)).astype(bf16)
                    )
                g_q = dot(jnp.concatenate(scores, axis=1), keys) * 0.125
                g_k = dot(jnp.concatenate(scores, axis=0), queries, TN)
                g_v = dot(jnp.concatenate(weights, axis=0), grad_two, TN)
                packed[0, p, rows, :] = g_q.astype(bf16)
                packed[1, p, rows, :] = g_k.astype(bf16)
                packed[2, p, rows, :] = g_v.astype(bf16)
                acc_q[0, p] += column_sums(g_q)
                acc_q[1, p] += column_sums(g_v)
            return carry

        return body

    acc_q[...] = jnp.zeros_like(acc_q)

    def grad_qkv_half(half):
        def body(s, carry):
            wide = jnp.concatenate([packed[s, 2 * half], packed[s, 2 * half + 1]], axis=1)
            o = dot(normed[...], wide, TN).astype(bf16)
            for z in range(GRID_Z):
                for p in range(GRID_P):
                    d = z * 4 + p
                    for j in range(2):
                        p_qkv[half, z, p, pl.ds(pl.multiple_of(64 * s + 32 * j, 32), 32)] = o[
                            32 * d : 32 * d + 32, LANES * j : LANES * j + LANES
                        ]
            return carry

        return body

    lax.fori_loop(0, ROWS, attend_back(me.sib), 0)
    down_u.third()
    up_u.second()
    lax.fori_loop(0, 3, grad_qkv_half(me.sib), 0)
    qkv_u.first()
    down_u.fourth()
    up_u.third()
    out_u.second()
    lax.fori_loop(0, ROWS, attend_back(me.h), 0)
    up_u.fourth()
    out_u.third()
    lax.fori_loop(0, 3, grad_qkv_half(me.h), 0)
    qkv_u.second()
    out_u.fourth()
    load_tok.wait()

    def grad_copy(i):
        return pltpu.make_async_copy(
            grad_stage.at[parity(i)], grad_hbm.at[block(i, BM), :], out_sem.at[2 + parity(i)]
        )

    def norm_one_back(i, carry):
        r = block(i, BM)

        @pl.when(i >= 2)
        def _():
            grad_copy(i - 2).wait()

        e = dot(tiles(packed.at[0], r), w_qkv[0].reshape(D, D), NT)
        e = e + dot(tiles(packed.at[1], r), w_qkv[1].reshape(D, D), NT)
        e = e + dot(tiles(packed.at[2], r), w_qkv[2].reshape(D, D), NT)
        xhat, rstd = normalized(tok[r, :].astype(f32))
        grad_stage[parity(i)] = gbr[r, :].astype(f32) + norm_back(e, xhat, rstd, gb[0:1, :])
        grad_copy(i).start()
        acc[0] += column_sums(e * xhat)
        acc[2] += column_sums(e)

        @pl.when(i == 2)
        def _():
            qkv_u.third()

        @pl.when(i == 6)
        def _():
            qkv_u.fourth()

        return carry

    lax.fori_loop(0, count, norm_one_back, 0)
    for p in range(4):
        acc[3, :, LANES * p : LANES * p + LANES] = acc_q[0, p]
        acc[4, :, LANES * p : LANES * p + LANES] = acc_q[1, p]
    for z in range(GRID_Z):
        rows = [jnp.sum(acc[n, :, LANES * z : LANES * z + LANES], axis=0, keepdims=True) for n in range(8)]
        rows += [
            jnp.sum(acc_up[:, 512 * z + LANES * p : 512 * z + LANES * p + LANES], axis=0, keepdims=True)
            for p in range(GRID_P)
        ]
        rows += [jnp.zeros((4, LANES), f32)]
        p_small[z] = jnp.concatenate(rows, axis=0)
    small_sum = SmallScatter(me, p_small, small_line, small_sets, s_send.at[4], s_recv.at[4])
    small_sum.first()
    total = down_u.fifth()
    for j in range(4):
        g_down[:, LANES * j : LANES * j + LANES] = total[64 * j : 64 * j + 64]
    total = up_u.fifth()
    for j in range(16):
        g_up[:, LANES * j : LANES * j + LANES] = total[16 * j : 16 * j + 16]
    small_sum.second()
    total = out_u.fifth()
    for j in range(2):
        g_out[:, LANES * j : LANES * j + LANES] = total[32 * j : 32 * j + 32]
    total = qkv_u.fifth()
    for s in range(3):
        for j in range(2):
            g_qkv[s, :, LANES * j : LANES * j + LANES] = total[64 * s + 32 * j : 64 * s + 32 * j + 32]
    small_sum.third(g_gains, g_biases, g_up_bias)
    for i in (count - 2, count - 1):
        out_copy(i).wait()
        grad_copy(i).wait()
    for item in big + units + [small, small_sum]:
        item.close()


def layer(tokens, cotangent, qkv, out, up, down, gains, biases, up_bias, segment, kinds):
    shape = jax.ShapeDtypeStruct
    T = tokens.shape[0]
    rows = T // SEQ
    outs = (
        shape((T, D), bf16),
        shape((T, D), f32),
        shape((3, 32, 256), f32),
        shape((32, 256), f32),
        shape((16, 2048), f32),
        shape((64, 512), f32),
        shape((2, 16), f32),
        shape((6, 16), f32),
        shape((1, 64), f32),
    )
    sizes = [256, 256, 64, 192]
    BM = 256
    V, S = pltpu.VMEM, pltpu.SemaphoreType.DMA
    scratch = [
        V((T, D), bf16), V((T, D), bf16),
        V((3, 4, 4, 32, 512), bf16), V((4, 4, 32, 512), bf16),
        V((4, 4, 2, 16, 2048), bf16), V((4, 4, 2, 64, 512), bf16),
        V((8, 512), f32), V((1, 2048), f32), V((rows, SEQ, SEQ), bf16),
        V((T, D), bf16), V((3, 4, T, LANES), bf16), V((rows, 8, SEQ, SEQ), bf16),
        V((4, T, LANES), bf16), V((T, 2048), bf16), V((T, 2048), bf16),
        V((T, D), bf16), V((4, T, LANES), bf16), V((8, 8, 512), f32), V((8, 2048), f32),
        V((2, 4, 8, LANES), f32),
        V((2, BM, D), bf16), V((2, BM, D), f32),
    ]
    scratch += [V((2, 4, 4, r, LANES), bf16) for r in sizes] + [V((4, 16, LANES), f32)]
    scratch += [V((4, 4, r, LANES), bf16) for r in sizes]
    scratch += [V((2, 2, r, LANES), bf16) for r in sizes]
    scratch += [V((2, 4, r, LANES), bf16) for r in sizes]
    scratch += [V((3, r, LANES), bf16) for r in sizes]
    scratch += [V((4, 4, 2, 16, LANES), bf16), V((3, 16, LANES), f32), V((8, 16, LANES), f32)]
    scratch += [S((7, 11)), S((7, 11)), S((6,)), S((5, 10)), S((5, 10)), S((2,)), S((4,))]
    return pl.pallas_call(
        layer_kernel,
        out_shape=outs,
        in_specs=[ANY] * 6 + [VM] * 5,
        out_specs=[ANY] * 2 + [VM] * 7,
        scratch_shapes=scratch,
        compiler_params=pltpu.CompilerParams(
            collective_id=0, has_side_effects=True, vmem_limit_bytes=VMEM_LIMIT
        ),
        name="layer",
    )(tokens, cotangent, qkv, out, up, down, gains, biases, up_bias, segment, kinds)


def widened(x, axes, dim):
    return lax.all_gather(x, axes, axis=dim, tiled=True)


def on_device(rep):
    def run(
        tokens, qkv, out, up, down, gains, biases, up_bias, segment, kinds, cotangent
    ):
        up_bias = up_bias.reshape(1, -1)
        head = lax.axis_index("head")
        if rep > 1:
            both = ("rep", "head")
            qkv, out = widened(qkv, "rep", 1), widened(out, "rep", 0)
            up = lax.dynamic_slice_in_dim(widened(up, both, 0), head * 16, 16, 0)
            down = lax.dynamic_slice_in_dim(widened(down, both, 0), head * 64, 64, 0)
            gains = lax.dynamic_slice_in_dim(widened(gains, both, 1), head * 16, 16, 1)
            biases = lax.dynamic_slice_in_dim(widened(biases, both, 1), head * 16, 16, 1)
            up_bias = lax.dynamic_slice_in_dim(widened(up_bias, both, 1), head * 64, 64, 1)
        output, grad, *grads = layer(
            tokens, cotangent, qkv, out, up, down, gains, biases, up_bias, segment, kinds
        )
        if rep > 1:
            place = lax.axis_index("rep") * 2 + head

            def own(x, dim):
                x = lax.all_gather(lax.psum(x, "rep"), "head", axis=dim, tiled=True)
                size = x.shape[dim] // (2 * rep)
                return lax.dynamic_slice_in_dim(x, place * size, size, dim)

            for i, dim in ((0, 1), (1, 0)):
                grads[i] = lax.psum_scatter(grads[i], "rep", scatter_dimension=dim, tiled=True)
            for i, dim in ((2, 0), (3, 0), (4, 1), (5, 1), (6, 1)):
                grads[i] = own(grads[i], dim)
        grads[6] = grads[6].reshape(-1)
        return (output, grad, *grads)

    return run


def solution(mesh):
    rep = mesh.shape["dp"] // (GRID_Z * GRID_P)
    wide = Mesh(mesh.devices.reshape(GRID_Z * GRID_P, rep, 2), ("dp", "rep", "head"))
    dp, every = ("dp", "rep"), ("dp", "rep", "head")
    in_specs = (
        P(every, None),
        P(None, dp, "head"),
        P(dp, "head"),
        P(every, None),
        P(every, None),
        P(None, every),
        P(None, every),
        P(every),
        P(dp, None),
        P(dp, None),
        P(every, None),
    )
    out_specs = (
        P(every, None),
        P(every, None),
        P(None, dp, "head"),
        P(dp, "head"),
        P(every, None),
        P(every, None),
        P(None, every),
        P(None, every),
        P(every),
    )
    return jax.shard_map(
        on_device(rep), mesh=wide, in_specs=in_specs, out_specs=out_specs, check_vma=False
    )
```

time: 1130 us -> 157 us (0.14); the launches traced: 1120 us -> 157 us
  waiting for transfers between devices: 483 us -> 0 us
  blocking collectives: 240 us -> 0 us
  matrix products: 186 us -> 0 us
  Pallas kernels: 0 us -> 146 us
  local copies, waits for them, and re-layouts: 125 us -> 9.48 us
  other arithmetic: 51.2 us -> 0 us
  between operations: 16.3 us -> 0.71 us
  starting transfers between devices: 13.8 us -> 0 us
    reduce_scatter x4 -> x0, waiting for transfers between devices: 287 us -> none  [the longest x1 140 us: on_device(): lax.psum_scatter(grad_down_part, ('dp', 'head'), scatter_dimension=0, til...]
    dot_general x68 -> x0, matrix products: 186 us -> none  [the longest x1 45 us: on_device(): jnp.dot(normed_two, up_full, preferred_element_type=jnp.float32)]
    all_gather x4 -> x0, blocking collectives: 162 us -> none  [the longest x1 43.8 us: on_device(): lax.all_gather(biases, ('dp', 'head'), axis=1, tiled=True)]
    unnamed x12 -> x0, waiting for transfers between devices: 148 us -> none
    pallas_call x0 -> x1, Pallas kernels: none -> 146 us  [layer(): pl.pallas_call(layer_kernel, out_shape=outs, in_specs=[ANY] * 6 + [VM] *...]
    unnamed x2 -> x0, blocking collectives: 77.8 us -> none
    reshape x4 -> x0, local copies, waits for them, and re-layouts: 41.8 us -> none  [the longest x1 18.7 us: on_device(): packed.reshape(block_count, block_rows, SEQ, 3, head_count, HEAD_DIM)]
    all_gather x4 -> x0, waiting for transfers between devices: 41 us -> none  [the longest x1 14.8 us: on_device(): lax.all_gather(up_weight, ('dp', 'head'), axis=0, tiled=True)]
  transfers between devices with their start and end apart: 12 -> 0, of which waited for: 9 -> 0; matrix products, arithmetic and copies ran while one was open for 10% -> 0% of each run, Pallas kernels for 0% -> 0%
where the time goes in v1:
time: 157 us
  Pallas kernels  146 us (93%)
  local copies, waits for them, and re-layouts  9.48 us (6%)
    pallas_call x1, Pallas kernels, layer(): pl.pallas_call(layer_kernel, out_shape=outs, in_specs=[ANY] * 6 + [VM] *...  146 us
    unnamed x25, local copies, waits for them, and re-layouts  9.48 us

profile of v1, /device:TPU:0, one launch (start us, length us, event | category | flops | bytes accessed | tf_op | source)
XLA Modules:
  0.0 156.6 jit_solution(4080460082215263579)
XLA Ops:
  0.6 146.5 %layer.1 = (bf16[2048,512]{1,0:T(8,128)(2,1)}, f32[2048,512]{1,0:T(8,128)}, f32[3,32,256]{2,1,0:T(8,128)}, f32[32,256]{1,0:T(8,128)}, f32[16,2048]{1,0:T(8,128)}...) custom-call(bf16[2048,512]{1,0:T(8,128)(2,1)} %tokens_hbm.1, ...), custom_call_target="tpu_custom_call" | custom-call | tf_op jit(solution)/shard_map/layer/pallas_call | solution.py:794
  147.1 0.0 copy-start
  147.1 3.2 %copy.29 = bf16[2048,512]{1,0:T(8,128)(2,1)} copy(bf16[2048,512]{1,0:T(8,128)(2,1)} %get-tuple-element.36) | data formatting | bytes 4194304
  150.3 0.0 copy-done
  150.3 0.0 copy-start.3
  150.3 0.0 copy-start.4
  150.3 0.0 copy-start.2
  150.3 0.0 copy-start.1
  150.3 0.0 copy-start.6
  150.4 0.0 copy-start.5
  150.4 0.0 copy-start.7
  150.4 2.0 %copy.30 = f32[2048,512]{1,0:T(8,128)} copy(f32[2048,512]{1,0:T(8,128)S(1)} %copy-done) | data formatting | bytes 8388608
  152.4 0.0 copy-done.3
  152.4 0.6 copy.31
  153.0 0.0 copy-done.4
  153.0 0.6 copy.32
  153.7 0.0 copy-done.2
  153.7 0.7 copy.33
  154.3 0.0 copy-done.1
  154.3 0.7 copy.34
  155.0 0.0 copy-done.6
  155.0 0.6 copy.35
  155.5 0.0 copy-done.5
  155.5 0.6 copy.36
  156.1 0.0 copy-done.7
  156.1 0.5 copy.37
Async XLA Ops:
  147.1 3.2 %copy-start = (f32[2048,512]{1,0:T(8,128)S(1)}, f32[2048,512]{1,0:T(8,128)}, u32[]{:S(2)}) copy-start(f32[2048,512]{1,0:T(8,128)} %get-tuple-element.37) | copy-start | bytes 12582916
  150.3 2.1 %copy-start.3 = (f32[3,32,256]{2,1,0:T(8,128)S(1)}, f32[3,32,256]{2,1,0:T(8,128)}, u32[]{:S(2)}) copy-start(f32[3,32,256]{2,1,0:T(8,128)} %get-tuple-element.38) | copy-start | bytes 294916
  150.3 2.7 %copy-start.4 = (f32[32,256]{1,0:T(8,128)S(1)}, f32[32,256]{1,0:T(8,128)}, u32[]{:S(2)}) copy-start(f32[32,256]{1,0:T(8,128)} %get-tuple-element.39) | copy-start | bytes 98308
  150.3 3.3 %copy-start.2 = (f32[16,2048]{1,0:T(8,128)S(1)}, f32[16,2048]{1,0:T(8,128)}, u32[]{:S(2)}) copy-start(f32[16,2048]{1,0:T(8,128)} %get-tuple-element.40) | copy-start | bytes 393220
  150.3 4.0 %copy-start.1 = (f32[64,512]{1,0:T(8,128)S(1)}, f32[64,512]{1,0:T(8,128)}, u32[]{:S(2)}) copy-start(f32[64,512]{1,0:T(8,128)} %get-tuple-element.41) | copy-start | bytes 393220
  150.3 4.6 %copy-start.6 = (f32[2,16]{1,0:T(2,128)S(1)}, f32[2,16]{1,0:T(2,128)}, u32[]{:S(2)}) copy-start(f32[2,16]{1,0:T(2,128)} %get-tuple-element.42) | copy-start | bytes 388
  150.4 5.2 %copy-start.5 = (f32[6,16]{1,0:T(8,128)S(1)}, f32[6,16]{1,0:T(8,128)}, u32[]{:S(2)}) copy-start(f32[6,16]{1,0:T(8,128)} %get-tuple-element.43) | copy-start | bytes 1156
  150.4 5.8 %copy-start.7 = (f32[1,64]{1,0:T(1,128)S(1)}, f32[1,64]{1,0:T(1,128)}, u32[]{:S(2)}) copy-start(f32[1,64]{1,0:T(1,128)} %get-tuple-element.26) | copy-start | bytes 772

commit v2 on v1

--- a/solution.py
+++ b/solution.py
@@ -52,6 +52,8 @@
         return lax.rem(self.z + k, GRID_Z)
 
     def line_back(self, k):
+        if k == 0:
+            return self.z
         return lax.rem(self.z + (GRID_Z - k), GRID_Z)
 
     def plane(self):
@@ -141,6 +143,64 @@
     def close(self):
         for make in self.started:
             make().wait_send()
+
+
+class PieceGather(Gather):
+    def first(self):
+        me = self.me
+        own = lambda: self.set_of(me.z, me.p)
+        self.mine = pltpu.make_async_copy(self.shard, own(), self.local)
+        self.mine.start()
+        for k in (1, 2, 3):
+            self.go(k - 1, lambda k=k: (self.shard, own(), me.at(me.line(k), me.p, me.h)))
+        self.go(3, lambda: (self.shard, own(), me.at(me.z, me.px, me.h)))
+        self.go(7, lambda: (self.shard, own(), me.at(me.z, me.py, me.h)))
+
+    def relay(self, k):
+        me = self.me
+        piece = lambda: self.set_of(me.line_back(k), me.p)
+        self.landed(k - 1, piece())
+        self.go(3 + k, lambda: (piece(), piece(), me.at(me.z, me.px, me.h)))
+        self.go(7 + k, lambda: (piece(), piece(), me.at(me.z, me.py, me.h)))
+
+    def forward(self, k):
+        me = self.me
+        x, y = lambda: self.set_of(me.line_back(k), me.px), lambda: self.set_of(me.line_back(k), me.py)
+        if k < 2:
+            self.landed(3 + k, x())
+            self.go(11 + k, lambda: (x(), x(), me.at(me.z, me.py, me.h)))
+        else:
+            self.landed(7 + k, y())
+            self.go(11 + k, lambda: (y(), y(), me.at(me.z, me.px, me.h)))
+
+    def across(self, index, p):
+        me = self.me
+        group = lambda: self.set_of(pl.ds(0, 4), p)
+        self.go(index, lambda: (group(), group(), me.at(me.z, me.p, me.sib)))
+
+    def own_across(self):
+        self.mine.wait()
+        self.across(15, self.me.p)
+
+    def neighbours_across(self):
+        me = self.me
+        for k in (2, 3):
+            self.landed(3 + k, self.set_of(me.line_back(k), me.px))
+        self.across(16, me.px)
+        for k in (0, 1):
+            self.landed(7 + k, self.set_of(me.line_back(k), me.py))
+        self.across(17, me.py)
+
+    def diagonal_across(self):
+        me = self.me
+        for k in range(4):
+            self.landed(11 + k, self.set_of(me.line_back(k), me.pd))
+        self.across(18, me.pd)
+
+    def fifth(self):
+        me = self.me
+        for index, p in ((15, me.p), (16, me.px), (17, me.py), (18, me.pd)):
+            self.landed(index, self.view(pl.ds(0, 4), p, me.sib))
 
 
 class SmallGather:
@@ -183,28 +243,28 @@
             ],
             axis=0,
         )
-        self.tiles[me.z, me.p, me.h] = rows.astype(bf16)
+        self.tiles[me.p, me.h, me.z] = rows.astype(bf16)
 
     def second(self):
         me = self.me
+        for k in (1, 2, 3):
+            self.go(k - 1, lambda k=k: (self.tiles.at[me.p, me.h, me.z], me.at(me.line(k), me.p, me.h)))
+
+    def third(self):
+        me = self.me
+        for k in (1, 2, 3):
+            self.landed(k - 1, self.tiles.at[me.p, me.h, me.line_back(k)])
         for index, (p, h) in enumerate(me.plane()):
-            self.go(index, lambda p=p, h=h: (self.tiles.at[me.z, me.p, me.h], me.at(me.z, p, h)))
-
-    def third(self):
+            self.go(3 + index, lambda p=p, h=h: (self.tiles.at[me.p, me.h], me.at(me.z, p, h)))
+
+    def fourth(self, gain_bias, up_bias):
         me = self.me
         for index, (p, h) in enumerate(me.plane()):
-            self.landed(index, self.tiles.at[me.z, p, h])
-        for k in (1, 2, 3):
-            self.go(6 + k, lambda k=k: (self.tiles.at[me.z], me.at(me.line(k), me.p, me.h)))
-
-    def fourth(self, gain_bias, up_bias):
-        me = self.me
-        for k in (1, 2, 3):
-            self.landed(6 + k, self.tiles.at[me.line_back(k)])
+            self.landed(3 + index, self.tiles.at[p, h])
         for z in range(GRID_Z):
             total = jnp.zeros((8, LANES), f32)
             for p in range(GRID_P):
-                pair = self.tiles[z, p, 0].astype(f32) + self.tiles[z, p, 1].astype(f32)
+                pair = self.tiles[p, 0, z].astype(f32) + self.tiles[p, 1, z].astype(f32)
                 total = total + pair[:8]
                 up_bias[:, (z * GRID_P + p) * LANES : (z * GRID_P + p + 1) * LANES] = pair[8:9]
             gain_bias[:, z * LANES : (z + 1) * LANES] = total
@@ -398,7 +458,7 @@
     for r in range(s.shape[0]):
         seg_j = jnp.broadcast_to(seg[r : r + 1], (SEQ, SEQ))
         run_j = jnp.broadcast_to(run[r : r + 1], (SEQ, SEQ))
-        mask[r] = jnp.where((seg_j.T == seg_j) & (run_j <= run_j.T), 0.0, -jnp.inf).astype(bf16)
+        mask[r] = jnp.where((seg_j.T == seg_j) & (run_j.T <= run_j), 0.0, -jnp.inf).astype(bf16)
 
 
 def layer_kernel(
@@ -407,46 +467,66 @@
     tok, cot, w_qkv, w_out, w_up, w_down, gb, upb, mask,
     normed, packed, att, mix, hid, gpre, gbr, gmix, acc, acc_up, acc_q,
     out_stage, grad_stage,
-    p_down, p_up, p_out, p_qkv, p_small,
-    core0, core1, core2, core3, cross0, cross1, cross2, cross3,
-    sets0, sets1, sets2, sets3, line0, line1, line2, line3,
+    p_down0, p_down1, p_up0, p_up1, p_out, p_qkv, p_small,
+    core0, core1, core2, core3, core4, core5, cross0, cross1, cross2, cross3, cross4, cross5,
+    sets0, sets1, sets2, sets3, sets4, sets5, line0, line1, line2, line3, line4, line5,
     small_tiles, small_line, small_sets,
     g_send, g_recv, g_local, s_send, s_recv, io_sem, out_sem,
 ):
     T = tok.shape[0]
     ROWS = T // SEQ
+    BM = out_stage.shape[1]
+    count = T // BM
     me = Place()
     load_tok = pltpu.make_async_copy(tokens_hbm, tok, io_sem.at[0])
     load_cot = pltpu.make_async_copy(cot_hbm, cot, io_sem.at[1])
     load_tok.start()
     load_cot.start()
 
-    def qkv_view(s):
-        return lambda z, p, h: w_qkv.at[s, z, p, :, pl.ds(pl.multiple_of(h * 256, 256), 256)]
-
-    views = [(qkv_s.at[s], qkv_view(s)) for s in range(3)]
-    views += [
-        (out_s, lambda z, p, h: w_out.at[z, p, :, pl.ds(pl.multiple_of(h * 256, 256), 256)]),
-        (up_s, lambda z, p, h: w_up.at[z, p, h]),
-        (down_s, lambda z, p, h: w_down.at[z, p, h]),
+    def columns(h):
+        return pl.ds(pl.multiple_of(h * 256, 256), 256)
+
+    def up_view(half):
+        return lambda z, p, h: w_up.at[z, p, h, :, pl.ds(1024 * half, 1024)]
+
+    def down_view(half):
+        return lambda z, p, h: w_down.at[z, p, h, pl.ds(32 * half, 32)]
+
+    views = [
+        (qkv_s, lambda z, p, h: w_qkv.at[:, z, p, :, columns(h)]),
+        (out_s, lambda z, p, h: w_out.at[z, p, :, columns(h)]),
+        (up_s.at[:, pl.ds(0, 1024)], up_view(0)),
+        (up_s.at[:, pl.ds(1024, 1024)], up_view(1)),
+        (down_s.at[pl.ds(0, 32)], down_view(0)),
+        (down_s.at[pl.ds(32, 32)], down_view(1)),
     ]
-    big = [
-        Gather(me, shard, view, g_send.at[i], g_recv.at[i], g_local.at[i])
+    gathers = [
+        (PieceGather if i == 0 else Gather)(me, shard, view, g_send.at[i], g_recv.at[i], g_local.at[i])
         for i, (shard, view) in enumerate(views)
     ]
-    attn_w, mlp_w = big[:3], big[3:]
+    qkv_g, out_g, up_a, up_b, down_a, down_b = gathers
     small = SmallGather(me, small_tiles, g_send.at[6], g_recv.at[6])
     small.first(gains, biases, up_bias)
     barrier(me)
     small.second()
-    for g in attn_w:
-        g.first()
+    qkv_g.first()
     own_rows = pl.ds(pl.multiple_of(me.h * ROWS, ROWS), ROWS)
     hidden_masks(segment[own_rows, :], kinds[own_rows, :], mask)
     small.third()
-    for g in attn_w:
-        g.second()
+    qkv_g.relay(1)
+    qkv_g.forward(0)
+    qkv_g.relay(2)
+    qkv_g.forward(1)
+    qkv_g.relay(3)
+    qkv_g.own_across()
+    out_g.first()
+    up_a.first()
     small.fourth(gb, upb)
+    qkv_g.forward(2)
+    qkv_g.forward(3)
+    qkv_g.neighbours_across()
+    up_b.first()
+    out_g.second()
     load_tok.wait()
 
     def norm_one(i, carry):
@@ -456,14 +536,19 @@
         return carry
 
     lax.fori_loop(0, T // 256, norm_one, 0)
-    for g in attn_w:
-        g.third()
-    for g in mlp_w:
-        g.first()
-    for g in attn_w:
-        g.fourth()
-    for g in attn_w:
-        g.fifth()
+    qkv_g.diagonal_across()
+    up_a.second()
+    down_a.first()
+    down_b.first()
+    qkv_g.fifth()
+
+    def at_step(i, steps):
+        for n, actions in steps.items():
+
+            @pl.when(i == n)
+            def _():
+                for action in actions:
+                    action()
 
     def project(i, carry):
         r = block(i, 512)
@@ -474,85 +559,82 @@
         for p in range(4):
             for s, value in enumerate((q, k, v)):
                 packed[s, p, r, :] = value[:, LANES * p : LANES * p + LANES]
+        at_step(i, {1: [up_b.second], 2: [out_g.third]})
         return carry
 
     lax.fori_loop(0, T // 512, project, 0)
-    for g in mlp_w:
-        g.second()
 
     def attend(i, carry):
-        for r in (2 * i, 2 * i + 1):
-            rows = block(r, SEQ)
-            hide = mask[r].astype(f32)
-            for p in range(4):
-                keys, values = two_heads(packed[1, p, rows, :]), two_heads(packed[2, p, rows, :])
-                scores = dot(packed[0, p, rows, :], keys, NT)
-                weights = []
-                for h in range(2):
-                    t = scores[:, SEQ * h : SEQ * h + SEQ] + hide
-                    e = jnp.exp(t - jnp.max(t, axis=-1, keepdims=True))
-                    a = (e * (1.0 / jnp.sum(e, axis=-1, keepdims=True))).astype(bf16)
-                    att[r, 2 * p + h] = a
-                    weights.append(a)
-                mix[p, rows, :] = dot(jnp.concatenate(weights, axis=1), values).astype(bf16)
-
-        @pl.when(i == 3)
-        def _():
-            for g in mlp_w:
-                g.third()
-
-        @pl.when(i == 6)
-        def _():
-            for g in mlp_w:
-                g.fourth()
-
+        items = [(4 * i + u, p) for u in range(4) for p in range(4)]
+        scores = [dot(two_heads(packed[1, p, block(r, SEQ), :]), packed[0, p, block(r, SEQ), :], NT) for r, p in items]
+        weights = []
+        for (r, p), pair in zip(items, scores):
+            heads = []
+            for h in range(2):
+                t = pair[SEQ * h : SEQ * h + SEQ] + mask[r].astype(f32)
+                e = jnp.exp(t - jnp.max(t, axis=0, keepdims=True))
+                a = (e * (1.0 / jnp.sum(e, axis=0, keepdims=True))).astype(bf16)
+                att[r, 2 * p + h] = a
+                heads.append(a)
+            weights.append(jnp.concatenate(heads, axis=0))
+        for (r, p), pair in zip(items, weights):
+            mix[p, block(r, SEQ), :] = dot(pair, two_heads(packed[2, p, block(r, SEQ), :]), TN).astype(bf16)
+        at_step(i, {0: [up_a.third], 1: [out_g.fourth, down_a.second], 2: [up_b.third], 3: [down_b.second, up_a.fourth]})
         return carry
 
-    lax.fori_loop(0, ROWS // 2, attend, 0)
+    lax.fori_loop(0, ROWS // 4, attend, 0)
+    out_g.fifth()
+
+    def middle_of(r):
+        return tok[r, :].astype(f32) + dot(tiles(mix, r), w_out[...].reshape(D, D), NT) + gb[5:6, :]
+
+    def norm_two(i, carry):
+        r = block(i, 512)
+        middle = middle_of(r)
+        xhat, _ = normalized(middle)
+        tok[r, :] = (xhat * gb[1:2, :] + gb[6:7, :]).astype(bf16)
+        middle = middle.astype(bf16)
+        for p in range(4):
+            gmix[p, r, :] = middle[:, LANES * p : LANES * p + LANES]
+        return carry
+
+    lax.fori_loop(0, T // 512, norm_two, 0)
+    up_b.fourth()
+    up_a.fifth()
+    up_b.fifth()
+
+    def hidden_block(i, carry):
+        r = block(i, BM)
+        two = tok[r, :]
+        for j in range(4):
+            cols = slice(512 * j, 512 * j + 512)
+            u = dot(two, w_up[:, :, :, :, cols].reshape(D, 512)) + upb[:, cols]
+            hidden, slope = gelu_and_slope(u)
+            hid[r, cols] = hidden.astype(bf16)
+            gpre[r, cols] = slope.astype(bf16)
+        at_step(i, {1: [down_a.third], 3: [down_b.third], 5: [down_a.fourth], 7: [down_b.fourth]})
+        return carry
+
+    lax.fori_loop(0, count, hidden_block, 0)
     load_cot.wait()
-    for g in mlp_w:
-        g.fifth()
-
+    down_a.fifth()
+    down_b.fifth()
     acc[...] = jnp.zeros_like(acc)
     acc_up[...] = jnp.zeros_like(acc_up)
-    BM = out_stage.shape[1]
-
-    def out_copy(i):
-        return pltpu.make_async_copy(
-            out_stage.at[parity(i)], output_hbm.at[block(i, BM), :], out_sem.at[parity(i)]
-        )
-
-    def feed_forward(i, carry):
+    acc_q[...] = jnp.zeros_like(acc_q)
+
+    def hidden_back(i, carry):
         r = block(i, BM)
-
-        @pl.when(i >= 2)
-        def _():
-            out_copy(i - 2).wait()
-
-        middle = tok[r, :].astype(f32) + dot(tiles(mix, r), w_out[...].reshape(D, D), NT) + gb[5:6, :]
-        xhat, rstd = normalized(middle)
-        two = (xhat * gb[1:2, :] + gb[6:7, :]).astype(bf16)
-        tok[r, :] = two
         c = cot[r, :]
-        total = middle + gb[7:8, :]
         e = jnp.zeros((BM, D), f32)
         for j in range(4):
             cols = slice(512 * j, 512 * j + 512)
-            w_up_j = w_up[:, :, :, :, cols].reshape(D, 512)
-            w_down_j = w_down[j].reshape(512, D)
-            u = dot(two, w_up_j) + upb[:, cols]
-            grad_hidden = dot(c, w_down_j, NT)
-            hidden, slope = gelu_and_slope(u)
-            hidden = hidden.astype(bf16)
-            hid[r, cols] = hidden
-            total = total + dot(hidden, w_down_j)
-            grad_pre = grad_hidden * slope
+            grad_pre = dot(c, w_down[j].reshape(512, D), NT) * gpre[r, cols].astype(f32)
             acc_up[:, cols] += column_sums(grad_pre)
             grad_pre = grad_pre.astype(bf16)
             gpre[r, cols] = grad_pre
-            e = e + dot(grad_pre, w_up_j, NT)
-        out_stage[parity(i)] = total.astype(bf16)
-        out_copy(i).start()
+            e = e + dot(grad_pre, w_up[:, :, :, :, cols].reshape(D, 512), NT)
+        xhat, rstd = normalized(tiles(gmix, r).astype(f32))
         cot_f32 = c.astype(f32)
         branch = (cot_f32 + norm_back(e, xhat, rstd, gb[1:2, :])).astype(bf16)
         gbr[r, :] = branch
@@ -565,52 +647,65 @@
         acc[7] += column_sums(cot_f32)
         return carry
 
-    count = T // BM
-    lax.fori_loop(0, count, feed_forward, 0)
+    lax.fori_loop(0, count, hidden_back, 0)
 
     units = [
         Scatter(me, *refs, s_send.at[i], s_recv.at[i])
         for i, refs in enumerate(
             (
-                (p_down, core0, cross0, sets0, line0),
-                (p_up, core1, cross1, sets1, line1),
-                (p_out, core2, cross2, sets2, line2),
-                (p_qkv, core3, cross3, sets3, line3),
+                (p_down0, core0, cross0, sets0, line0),
+                (p_down1, core1, cross1, sets1, line1),
+                (p_up0, core2, cross2, sets2, line2),
+                (p_up1, core3, cross3, sets3, line3),
+                (p_out, core4, cross4, sets4, line4),
+                (p_qkv, core5, cross5, sets5, line5),
             )
         )
     ]
-    down_u, up_u, out_u, qkv_u = units
-
-    def grad_down_chunk(z, carry):
-        o = dot(hid[:, block(z, 512)], cot[...], TN).astype(bf16)
-        for p in range(GRID_P):
-            for h in range(2):
-                for j in range(4):
-                    p_down[h, z, p, 64 * j : 64 * j + 64] = o[
-                        64 * (2 * p + h) : 64 * (2 * p + h) + 64, LANES * j : LANES * j + LANES
-                    ]
-        return carry
-
-    lax.fori_loop(0, 4, grad_down_chunk, 0)
-    down_u.first()
-
-    def grad_up_chunk(c, carry):
-        o = dot(tok[...], gpre[:, block(c, 512)], TN).astype(bf16)
-        for z in range(GRID_Z):
+    d0, d1, u0, u1, out_u, qkv_u = units
+
+    def grad_down_chunk(half, part):
+        def body(z, carry):
+            o = dot(cot[:, 256 * half : 256 * half + 256], hid[:, block(z, 512)], TN).astype(bf16).T
             for p in range(GRID_P):
                 for h in range(2):
-                    d = (z * 4 + p) * 2 + h
-                    for j in range(4):
-                        p_up[h, z, p, pl.ds(pl.multiple_of(64 * c + 16 * j, 16), 16)] = o[
-                            16 * d : 16 * d + 16, LANES * j : LANES * j + LANES
+                    for j in range(2):
+                        part[h, z, p, 64 * j : 64 * j + 64] = o[
+                            64 * (2 * p + h) : 64 * (2 * p + h) + 64, LANES * j : LANES * j + LANES
                         ]
-        return carry
-
-    lax.fori_loop(0, 4, grad_up_chunk, 0)
-    up_u.first()
+            return carry
+
+        return body
+
+    def grad_up_chunk(half, part):
+        def body(c, carry):
+            o = dot(tok[...], gpre[:, block(2 * half + c, 512)], TN).astype(bf16)
+            for z in range(GRID_Z):
+                for p in range(GRID_P):
+                    for h in range(2):
+                        d = (z * 4 + p) * 2 + h
+                        for j in range(4):
+                            part[h, z, p, pl.ds(pl.multiple_of(64 * c + 16 * j, 16), 16)] = o[
+                                16 * d : 16 * d + 16, LANES * j : LANES * j + LANES
+                            ]
+            return carry
+
+        return body
+
+    lax.fori_loop(0, 4, grad_down_chunk(0, p_down0), 0)
+    d0.first()
+    lax.fori_loop(0, 4, grad_down_chunk(1, p_down1), 0)
+    d1.first()
+    d0.second()
+    lax.fori_loop(0, 2, grad_up_chunk(0, p_up0), 0)
+    u0.first()
+    d1.second()
+    lax.fori_loop(0, 2, grad_up_chunk(1, p_up1), 0)
+    u1.first()
     load_tok = pltpu.make_async_copy(tokens_hbm, tok, io_sem.at[0])
     load_tok.start()
-    down_u.second()
+    u0.second()
+    d0.third()
 
     o = dot(gbr[...], jnp.concatenate([mix[p] for p in range(4)], axis=1), TN).astype(bf16)
     for z in range(GRID_Z):
@@ -622,40 +717,45 @@
                         32 * d : 32 * d + 32, 256 * h + LANES * j : 256 * h + LANES * j + LANES
                     ]
     out_u.first()
-
-    def attend_back(half):
-        def body(r, carry):
-            rows = block(r, SEQ)
-            for pp in range(2):
-                p = 2 * half + pp
+    u1.second()
+    d1.third()
+
+    def attend_back(half, steps):
+        def body(i, carry):
+            row = lax.broadcasted_iota(jnp.int32, (2 * SEQ, LANES), 0) // SEQ
+            lane = lax.broadcasted_iota(jnp.int32, (2 * SEQ, LANES), 1) // 64
+            minus = jnp.where(row == lane, -1.0, 0.0).astype(bf16)
+            items = [(4 * i + u, 2 * half + pp) for u in range(4) for pp in range(2)]
+            grads, slopes = [], []
+            for r, p in items:
+                rows = block(r, SEQ)
+                grad = gmix[p, rows, :]
+                product = (grad.astype(f32) * mix[p, rows, :].astype(f32)).astype(bf16)
+                values = jnp.concatenate([two_heads(packed[2, p, rows, :]), minus], axis=1)
+                grads.append(dot(values, jnp.concatenate([grad, product], axis=1), NT))
+            for (r, p), pair in zip(items, grads):
+                slopes.append(
+                    [
+                        (att[r, 2 * p + h].astype(f32) * pair[SEQ * h : SEQ * h + SEQ]).astype(bf16)
+                        for h in range(2)
+                    ]
+                )
+            for (r, p), pair in zip(items, slopes):
+                rows = block(r, SEQ)
                 queries, keys = two_heads(packed[0, p, rows, :]), two_heads(packed[1, p, rows, :])
-                values = two_heads(packed[2, p, rows, :])
-                grad = gmix[p, rows, :]
-                grad_two = two_heads(grad)
-                grad_weight = dot(grad, values, NT)
-                product = grad.astype(f32) * mix[p, rows, :].astype(f32)
-                first = lax.broadcasted_iota(jnp.int32, (SEQ, LANES), 1) < 64
-                scores, weights = [], []
-                for h in range(2):
-                    inner = jnp.sum(jnp.where(first == (h == 0), product, 0.0), axis=-1, keepdims=True)
-                    a = att[r, 2 * p + h]
-                    weights.append(a)
-                    scores.append(
-                        (a.astype(f32) * (grad_weight[:, SEQ * h : SEQ * h + SEQ] - inner)).astype(bf16)
-                    )
-                g_q = dot(jnp.concatenate(scores, axis=1), keys) * 0.125
-                g_k = dot(jnp.concatenate(scores, axis=0), queries, TN)
-                g_v = dot(jnp.concatenate(weights, axis=0), grad_two, TN)
+                g_q = dot(jnp.concatenate(pair, axis=0), keys, TN) * 0.125
+                g_k = dot(jnp.concatenate(pair, axis=1), queries)
+                weights = jnp.concatenate([att[r, 2 * p], att[r, 2 * p + 1]], axis=1)
+                g_v = dot(weights, two_heads(gmix[p, rows, :]))
                 packed[0, p, rows, :] = g_q.astype(bf16)
                 packed[1, p, rows, :] = g_k.astype(bf16)
                 packed[2, p, rows, :] = g_v.astype(bf16)
                 acc_q[0, p] += column_sums(g_q)
                 acc_q[1, p] += column_sums(g_v)
+            at_step(i, steps)
             return carry
 
         return body
-
-    acc_q[...] = jnp.zeros_like(acc_q)
 
     def grad_qkv_half(half):
         def body(s, carry):
@@ -672,19 +772,15 @@
 
         return body
 
-    lax.fori_loop(0, ROWS, attend_back(me.sib), 0)
-    down_u.third()
-    up_u.second()
+    lax.fori_loop(0, ROWS // 4, attend_back(me.sib, {0: [u0.third], 1: [d0.fourth], 3: [out_u.second]}), 0)
     lax.fori_loop(0, 3, grad_qkv_half(me.sib), 0)
     qkv_u.first()
-    down_u.fourth()
-    up_u.third()
-    out_u.second()
-    lax.fori_loop(0, ROWS, attend_back(me.h), 0)
-    up_u.fourth()
-    out_u.third()
+    u1.third()
+    d1.fourth()
+    lax.fori_loop(0, ROWS // 4, attend_back(me.h, {1: [out_u.third], 2: [u0.fourth]}), 0)
     lax.fori_loop(0, 3, grad_qkv_half(me.h), 0)
     qkv_u.second()
+    u1.fourth()
     out_u.fourth()
     load_tok.wait()
 
@@ -708,15 +804,7 @@
         grad_copy(i).start()
         acc[0] += column_sums(e * xhat)
         acc[2] += column_sums(e)
-
-        @pl.when(i == 2)
-        def _():
-            qkv_u.third()
-
-        @pl.when(i == 6)
-        def _():
-            qkv_u.fourth()
-
+        at_step(i, {5: [qkv_u.third]})
         return carry
 
     lax.fori_loop(0, count, norm_one_back, 0)
@@ -731,28 +819,74 @@
         ]
         rows += [jnp.zeros((4, LANES), f32)]
         p_small[z] = jnp.concatenate(rows, axis=0)
-    small_sum = SmallScatter(me, p_small, small_line, small_sets, s_send.at[4], s_recv.at[4])
+    small_sum = SmallScatter(me, p_small, small_line, small_sets, s_send.at[6], s_recv.at[6])
     small_sum.first()
-    total = down_u.fifth()
-    for j in range(4):
-        g_down[:, LANES * j : LANES * j + LANES] = total[64 * j : 64 * j + 64]
-    total = up_u.fifth()
-    for j in range(16):
-        g_up[:, LANES * j : LANES * j + LANES] = total[16 * j : 16 * j + 16]
-    small_sum.second()
+
+    def out_copy(i):
+        return pltpu.make_async_copy(
+            out_stage.at[parity(i)], output_hbm.at[block(i, BM), :], out_sem.at[parity(i)]
+        )
+
+    def output_block(i, carry):
+        r = block(i, BM)
+
+        @pl.when(i >= 2)
+        def _():
+            out_copy(i - 2).wait()
+
+        total = middle_of(r) + dot(hid[r, :], w_down[...].reshape(2048, D)) + gb[7:8, :]
+        out_stage[parity(i)] = total.astype(bf16)
+        out_copy(i).start()
+        at_step(i, {3: [small_sum.second, qkv_u.fourth]})
+        return carry
+
+    lax.fori_loop(0, count, output_block, 0)
+    for unit, j0 in ((d0, 0), (d1, 2)):
+        total = unit.fifth()
+        for j in range(2):
+            g_down[:, LANES * (j0 + j) : LANES * (j0 + j) + LANES] = total[64 * j : 64 * j + 64]
+    for unit, j0 in ((u0, 0), (u1, 8)):
+        total = unit.fifth()
+        for j in range(8):
+            g_up[:, LANES * (j0 + j) : LANES * (j0 + j) + LANES] = total[16 * j : 16 * j + 16]
     total = out_u.fifth()
     for j in range(2):
         g_out[:, LANES * j : LANES * j + LANES] = total[32 * j : 32 * j + 32]
+    small_sum.third(g_gains, g_biases, g_up_bias)
     total = qkv_u.fifth()
     for s in range(3):
         for j in range(2):
             g_qkv[s, :, LANES * j : LANES * j + LANES] = total[64 * s + 32 * j : 64 * s + 32 * j + 32]
-    small_sum.third(g_gains, g_biases, g_up_bias)
     for i in (count - 2, count - 1):
         out_copy(i).wait()
         grad_copy(i).wait()
-    for item in big + units + [small, small_sum]:
+    for item in gathers + units + [small, small_sum]:
         item.close()
+
+
+def finish_kernel(*refs):
+    for source, target in zip(refs[:9], refs[9:]):
+        target[...] = source[...]
+
+
+def finish(*arrays):
+    steps = 4
+
+    def spec(array, n):
+        if n < 2:
+            return pl.BlockSpec((array.shape[0] // steps, array.shape[1]), lambda i: (i, 0))
+        return pl.BlockSpec(array.shape, lambda i: (0,) * array.ndim)
+
+    specs = [spec(a, n) for n, a in enumerate(arrays)]
+    return pl.pallas_call(
+        finish_kernel,
+        out_shape=tuple(jax.ShapeDtypeStruct(a.shape, a.dtype) for a in arrays),
+        grid=(steps,),
+        in_specs=specs,
+        out_specs=specs,
+        compiler_params=pltpu.CompilerParams(vmem_limit_bytes=VMEM_LIMIT),
+        name="finish",
+    )(*arrays)
 
 
 def layer(tokens, cotangent, qkv, out, up, down, gains, biases, up_bias, segment, kinds):
@@ -770,7 +904,7 @@
         shape((6, 16), f32),
         shape((1, 64), f32),
     )
-    sizes = [256, 256, 64, 192]
+    sizes = [128, 128, 128, 128, 64, 192]
     BM = 256
     V, S = pltpu.VMEM, pltpu.SemaphoreType.DMA
     scratch = [
@@ -789,8 +923,8 @@
     scratch += [V((2, 2, r, LANES), bf16) for r in sizes]
     scratch += [V((2, 4, r, LANES), bf16) for r in sizes]
     scratch += [V((3, r, LANES), bf16) for r in sizes]
-    scratch += [V((4, 4, 2, 16, LANES), bf16), V((3, 16, LANES), f32), V((8, 16, LANES), f32)]
-    scratch += [S((7, 11)), S((7, 11)), S((6,)), S((5, 10)), S((5, 10)), S((2,)), S((4,))]
+    scratch += [V((4, 2, 4, 16, LANES), bf16), V((3, 16, LANES), f32), V((8, 16, LANES), f32)]
+    scratch += [S((7, 19)), S((7, 19)), S((6,)), S((7, 10)), S((7, 10)), S((2,)), S((4,))]
     return pl.pallas_call(
         layer_kernel,
         out_shape=outs,
@@ -822,8 +956,8 @@
             gains = lax.dynamic_slice_in_dim(widened(gains, both, 1), head * 16, 16, 1)
             biases = lax.dynamic_slice_in_dim(widened(biases, both, 1), head * 16, 16, 1)
             up_bias = lax.dynamic_slice_in_dim(widened(up_bias, both, 1), head * 64, 64, 1)
-        output, grad, *grads = layer(
-            tokens, cotangent, qkv, out, up, down, gains, biases, up_bias, segment, kinds
+        output, grad, *grads = finish(
+            *layer(tokens, cotangent, qkv, out, up, down, gains, biases, up_bias, segment, kinds)
         )
         if rep > 1:
             place = lax.axis_index("rep") * 2 + head

time: 157 us -> 126 us (0.80)
  Pallas kernels: 146 us -> 125 us
  local copies, waits for them, and re-layouts: 9.48 us -> 0 us
    pallas_call x1, Pallas kernels: 146 us -> 119 us  [layer(): pl.pallas_call(layer_kernel, out_shape=outs, in_specs=[ANY] * 6 + [VM] *...]
    unnamed x25 -> x0, local copies, waits for them, and re-layouts: 9.48 us -> none
    pallas_call x0 -> x1, Pallas kernels: none -> 6.15 us  [finish(): pl.pallas_call(finish_kernel, out_shape=tuple((jax.ShapeDtypeStruct(a.sha...]
where the time goes in v2:
time: 126 us
  Pallas kernels  125 us (99%)
    pallas_call x1, Pallas kernels, layer(): pl.pallas_call(layer_kernel, out_shape=outs, in_specs=[ANY] * 6 + [VM] *...  119 us
    pallas_call x1, Pallas kernels, finish(): pl.pallas_call(finish_kernel, out_shape=tuple((jax.ShapeDtypeStruct(a.sha...  6.15 us

profile of v2, /device:TPU:0, one launch (start us, length us, event | category | flops | bytes accessed | tf_op | source)
XLA Modules:
  0.0 125.5 jit_solution(9943147711707369293)
XLA Ops:
  0.6 118.5 %layer.1 = (bf16[2048,512]{1,0:T(8,128)(2,1)}, f32[2048,512]{1,0:T(8,128)}, f32[3,32,256]{2,1,0:T(8,128)}, f32[32,256]{1,0:T(8,128)}, f32[16,2048]{1,0:T(8,128)}...) custom-call(bf16[2048,512]{1,0:T(8,128)(2,1)} %tokens_hbm.1, ...), custom_call_target="tpu_custom_call" | custom-call | tf_op jit(solution)/shard_map/layer/pallas_call | solution.py:928
  119.2 6.2 %finish.1 = (bf16[2048,512]{1,0:T(8,128)(2,1)}, f32[2048,512]{1,0:T(8,128)}, f32[3,32,256]{2,1,0:T(8,128)}, f32[32,256]{1,0:T(8,128)}, f32[16,2048]{1,0:T(8,128)...) custom-call(bf16[2048,512]{1,0:T(8,128)(2,1)} %get-tuple-element.27.refs_0_, ...), custom_call_target="tpu_custom_call" | custom-call | tf_op jit(solution)/shard_map/finish/pallas_call | solution.py:881

commit v3 on v2

--- a/solution.py
+++ b/solution.py
@@ -18,6 +18,7 @@
 NN = (((1,), (0,)), ((), ()))
 NT = (((1,), (1,)), ((), ()))
 TN = (((0,), (0,)), ((), ()))
+DOWN_ROWS, UP_ROWS, OUT_ROWS, QKV_ROWS, SMALL_ROWS, ALL_ROWS = 0, 256, 512, 576, 768, 784
 VMEM_LIMIT = (63 << 20) + (512 << 10)
 
 
@@ -145,7 +146,10 @@
             make().wait_send()
 
 
-class PieceGather(Gather):
+class DirectGather(Gather):
+    def others(self):
+        return self.me.px, self.me.py, self.me.pd
+
     def first(self):
         me = self.me
         own = lambda: self.set_of(me.z, me.p)
@@ -153,25 +157,15 @@
         self.mine.start()
         for k in (1, 2, 3):
             self.go(k - 1, lambda k=k: (self.shard, own(), me.at(me.line(k), me.p, me.h)))
-        self.go(3, lambda: (self.shard, own(), me.at(me.z, me.px, me.h)))
-        self.go(7, lambda: (self.shard, own(), me.at(me.z, me.py, me.h)))
+        for n, p in enumerate(self.others()):
+            self.go(3 + 4 * n, lambda p=p: (self.shard, own(), me.at(me.z, p, me.h)))
 
     def relay(self, k):
         me = self.me
         piece = lambda: self.set_of(me.line_back(k), me.p)
         self.landed(k - 1, piece())
-        self.go(3 + k, lambda: (piece(), piece(), me.at(me.z, me.px, me.h)))
-        self.go(7 + k, lambda: (piece(), piece(), me.at(me.z, me.py, me.h)))
-
-    def forward(self, k):
-        me = self.me
-        x, y = lambda: self.set_of(me.line_back(k), me.px), lambda: self.set_of(me.line_back(k), me.py)
-        if k < 2:
-            self.landed(3 + k, x())
-            self.go(11 + k, lambda: (x(), x(), me.at(me.z, me.py, me.h)))
-        else:
-            self.landed(7 + k, y())
-            self.go(11 + k, lambda: (y(), y(), me.at(me.z, me.px, me.h)))
+        for n, p in enumerate(self.others()):
+            self.go(3 + 4 * n + k, lambda p=p: (piece(), piece(), me.at(me.z, p, me.h)))
 
     def across(self, index, p):
         me = self.me
@@ -182,20 +176,12 @@
         self.mine.wait()
         self.across(15, self.me.p)
 
-    def neighbours_across(self):
-        me = self.me
-        for k in (2, 3):
-            self.landed(3 + k, self.set_of(me.line_back(k), me.px))
-        self.across(16, me.px)
-        for k in (0, 1):
-            self.landed(7 + k, self.set_of(me.line_back(k), me.py))
-        self.across(17, me.py)
-
-    def diagonal_across(self):
-        me = self.me
+    def other_across(self, n):
+        me = self.me
+        p = self.others()[n]
         for k in range(4):
-            self.landed(11 + k, self.set_of(me.line_back(k), me.pd))
-        self.across(18, me.pd)
+            self.landed(3 + 4 * n + k, self.set_of(me.line_back(k), p))
+        self.across(16 + n, p)
 
     def fifth(self):
         me = self.me
@@ -203,11 +189,46 @@
             self.landed(index, self.view(pl.ds(0, 4), p, me.sib))
 
 
+class PlaneGather(Gather):
+    def group(self, z):
+        return self.view(z, pl.ds(0, 4), self.me.h)
+
+    def first(self):
+        me = self.me
+        own = lambda: self.set_of(me.z, me.p)
+        self.mine = pltpu.make_async_copy(self.shard, own(), self.local)
+        self.mine.start()
+        for n, p in enumerate((me.px, me.py, me.pd)):
+            self.go(n, lambda p=p: (self.shard, own(), me.at(me.z, p, me.h)))
+
+    def second(self):
+        me = self.me
+        self.mine.wait()
+        for n, p in enumerate((me.px, me.py, me.pd)):
+            self.landed(n, self.set_of(me.z, p))
+        for k in (1, 2, 3):
+            self.go(2 + k, lambda k=k: (self.group(me.z), self.group(me.z), me.at(me.line(k), me.p, me.h)))
+        self.go(6, lambda: (self.group(me.z), self.group(me.z), me.at(me.z, me.p, me.sib)))
+
+    def third(self):
+        me = self.me
+        for k in (1, 2, 3):
+            z = me.line_back(k)
+            self.landed(2 + k, self.group(z))
+            self.go(6 + k, lambda z=z: (self.group(z), self.group(z), me.at(me.z, me.p, me.sib)))
+
+    def fourth(self):
+        pass
+
+    def fifth(self):
+        me = self.me
+        for k in range(4):
+            self.landed(6 + k, self.view(me.line_back(k), pl.ds(0, 4), me.sib))
+
+
 class SmallGather:
-    SENDS, RECVS = 10, 10
-
-    def __init__(self, me, tiles, send, recv):
-        self.me, self.tiles, self.send, self.recv = me, tiles, send, recv
+    def __init__(self, me, tiles, lines, send, recv):
+        self.me, self.tiles, self.lines, self.send, self.recv = me, tiles, lines, send, recv
         self.started = []
 
     def go(self, index, parts):
@@ -234,40 +255,44 @@
             ).astype(bf16),
         )
         start = (me.p * 2 + me.h) * 16
+        row = lax.broadcasted_iota(jnp.int32, (8, LANES), 0)
+        hidden = jnp.broadcast_to(place(up_bias[...], 64, me.h * 64), (8, LANES))
         rows = jnp.concatenate(
             [
                 place(gains[...], 16, start),
                 place(biases[...], 16, start),
-                place(up_bias[...], 64, me.h * 64),
-                jnp.zeros((7, LANES), f32),
+                jnp.where(row == me.p, hidden, 0.0),
             ],
             axis=0,
         )
-        self.tiles[me.p, me.h, me.z] = rows.astype(bf16)
+        self.tiles[me.p, me.h] = rows.astype(bf16)
 
     def second(self):
         me = self.me
+        for index, (p, h) in enumerate(me.plane()):
+            self.go(index, lambda p=p, h=h: (self.tiles.at[me.p, me.h], me.at(me.z, p, h)))
+
+    def third(self):
+        me = self.me
+        for index, (p, h) in enumerate(me.plane()):
+            self.landed(index, self.tiles.at[p, h])
+        total = jnp.zeros((16, LANES), f32)
+        for p in range(GRID_P):
+            for h in range(2):
+                total = total + self.tiles[p, h].astype(f32)
+        self.lines[me.z] = total.astype(bf16)
         for k in (1, 2, 3):
-            self.go(k - 1, lambda k=k: (self.tiles.at[me.p, me.h, me.z], me.at(me.line(k), me.p, me.h)))
-
-    def third(self):
+            self.go(6 + k, lambda k=k: (self.lines.at[me.z], me.at(me.line(k), me.p, me.h)))
+
+    def fourth(self, gain_bias, up_bias):
         me = self.me
         for k in (1, 2, 3):
-            self.landed(k - 1, self.tiles.at[me.p, me.h, me.line_back(k)])
-        for index, (p, h) in enumerate(me.plane()):
-            self.go(3 + index, lambda p=p, h=h: (self.tiles.at[me.p, me.h], me.at(me.z, p, h)))
-
-    def fourth(self, gain_bias, up_bias):
-        me = self.me
-        for index, (p, h) in enumerate(me.plane()):
-            self.landed(3 + index, self.tiles.at[p, h])
+            self.landed(6 + k, self.lines.at[me.line_back(k)])
         for z in range(GRID_Z):
-            total = jnp.zeros((8, LANES), f32)
+            line = self.lines[z].astype(f32)
+            gain_bias[:, z * LANES : (z + 1) * LANES] = line[:8]
             for p in range(GRID_P):
-                pair = self.tiles[p, 0, z].astype(f32) + self.tiles[p, 1, z].astype(f32)
-                total = total + pair[:8]
-                up_bias[:, (z * GRID_P + p) * LANES : (z * GRID_P + p + 1) * LANES] = pair[8:9]
-            gain_bias[:, z * LANES : (z + 1) * LANES] = total
+                up_bias[:, (z * GRID_P + p) * LANES : (z * GRID_P + p + 1) * LANES] = line[8 + p : 9 + p]
 
     def close(self):
         for make in self.started:
@@ -301,13 +326,7 @@
     def second(self):
         me, part = self.me, self.part
         self.landed(0, self.core)
-
-        def add(i, carry):
-            z, p = i // GRID_P, lax.rem(i, GRID_P)
-            part[me.h, z, p] = (part[me.h, z, p].astype(f32) + self.core[z, p].astype(f32)).astype(bf16)
-            return carry
-
-        lax.fori_loop(0, GRID_Z * GRID_P, add, 0)
+        part[me.h] = part[me.h] + self.core[...]
         self.go(1, lambda: (part.at[me.h, pl.ds(0, 2), me.pd], self.cross.at[0], me.at(me.z, me.py, me.h)))
         self.go(2, lambda: (part.at[me.h, pl.ds(2, 2), me.pd], self.cross.at[1], me.at(me.z, me.px, me.h)))
 
@@ -317,10 +336,8 @@
         self.landed(2, self.cross.at[1])
 
         for i in range(2):
-            part[me.h, i, me.px] = (part[me.h, i, me.px].astype(f32) + self.cross[0, i].astype(f32)).astype(bf16)
-            part[me.h, 2 + i, me.py] = (
-                part[me.h, 2 + i, me.py].astype(f32) + self.cross[1, i].astype(f32)
-            ).astype(bf16)
+            part[me.h, i, me.px] = part[me.h, i, me.px] + self.cross[0, i]
+            part[me.h, 2 + i, me.py] = part[me.h, 2 + i, me.py] + self.cross[1, i]
         self.go(3, lambda: (part.at[me.h, :, me.px], self.sets.at[0], me.at(me.z, me.px, me.h)))
         self.go(4, lambda: (part.at[me.h, :, me.py], self.sets.at[1], me.at(me.z, me.py, me.h)))
 
@@ -393,19 +410,17 @@
                 3 + index, lambda i=index, p=p, h=h: (self.sets.at[7], self.sets.at[i], me.at(me.z, p, h))
             )
 
-    def third(self, gains, biases, up_bias):
+    def third(self, sums):
         me = self.me
         total = self.sets[7]
         for index in range(7):
             self.landed(3 + index, self.sets.at[index])
             total = total + self.sets[index]
-        rows = pltpu.roll(total[:8], LANES - 16 * (me.p * 2 + me.h), 1)
-        gains[...] = rows[0:2, 0:16]
-        biases[...] = rows[2:8, 0:16]
+        sums[SMALL_ROWS : SMALL_ROWS + 8] = pltpu.roll(total[:8], LANES - 16 * (me.p * 2 + me.h), 1)
         row = lax.broadcasted_iota(jnp.int32, (8, LANES), 0)
         hidden = jnp.sum(jnp.where(row == me.p, total[8:], 0.0), axis=0, keepdims=True)
-        hidden = jnp.where(me.h == 0, hidden[:, 0:64], hidden[:, 64:128])
-        up_bias[...] = hidden
+        hidden = jnp.broadcast_to(hidden, (8, LANES))
+        sums[SMALL_ROWS + 8 : SMALL_ROWS + 16] = jnp.where(me.h == 0, hidden, pltpu.roll(hidden, 64, 1))
 
     def close(self):
         for make in self.started:
@@ -463,28 +478,33 @@
 
 def layer_kernel(
     tokens_hbm, cot_hbm, qkv_s, out_s, up_s, down_s, gains, biases, up_bias, segment, kinds,
-    output_hbm, grad_hbm, g_qkv, g_out, g_up, g_down, g_gains, g_biases, g_up_bias,
+    output_hbm, grad_hbm, sums,
     tok, cot, w_qkv, w_out, w_up, w_down, gb, upb, mask,
     normed, packed, att, mix, hid, gpre, gbr, gmix, acc, acc_up, acc_q,
-    out_stage, grad_stage,
+    grad_stage,
     p_down0, p_down1, p_up0, p_up1, p_out, p_qkv, p_small,
     core0, core1, core2, core3, core4, core5, cross0, cross1, cross2, cross3, cross4, cross5,
     sets0, sets1, sets2, sets3, sets4, sets5, line0, line1, line2, line3, line4, line5,
-    small_tiles, small_line, small_sets,
+    small_tiles, small_lines, small_line, small_sets,
     g_send, g_recv, g_local, s_send, s_recv, io_sem, out_sem,
 ):
     T = tok.shape[0]
     ROWS = T // SEQ
-    BM = out_stage.shape[1]
+    BM = 256
     count = T // BM
+    BACK = grad_stage.shape[1]
+    back_count = T // BACK
     me = Place()
     load_tok = pltpu.make_async_copy(tokens_hbm, tok, io_sem.at[0])
     load_cot = pltpu.make_async_copy(cot_hbm, cot, io_sem.at[1])
     load_tok.start()
     load_cot.start()
 
-    def columns(h):
-        return pl.ds(pl.multiple_of(h * 256, 256), 256)
+    def columns(h, width=256):
+        return pl.ds(pl.multiple_of(h * width, width), width)
+
+    def qkv_view(c):
+        return lambda z, p, h: w_qkv.at[c, :, z, p, :, columns(h, LANES)]
 
     def up_view(half):
         return lambda z, p, h: w_up.at[z, p, h, :, pl.ds(1024 * half, 1024)]
@@ -493,7 +513,8 @@
         return lambda z, p, h: w_down.at[z, p, h, pl.ds(32 * half, 32)]
 
     views = [
-        (qkv_s, lambda z, p, h: w_qkv.at[:, z, p, :, columns(h)]),
+        (qkv_s.at[:, :, pl.ds(0, LANES)], qkv_view(0)),
+        (qkv_s.at[:, :, pl.ds(LANES, LANES)], qkv_view(1)),
         (out_s, lambda z, p, h: w_out.at[z, p, :, columns(h)]),
         (up_s.at[:, pl.ds(0, 1024)], up_view(0)),
         (up_s.at[:, pl.ds(1024, 1024)], up_view(1)),
@@ -501,32 +522,27 @@
         (down_s.at[pl.ds(32, 32)], down_view(1)),
     ]
     gathers = [
-        (PieceGather if i == 0 else Gather)(me, shard, view, g_send.at[i], g_recv.at[i], g_local.at[i])
+        (DirectGather if i < 2 else PlaneGather if i == 6 else Gather)(me, shard, view, g_send.at[i], g_recv.at[i], g_local.at[i])
         for i, (shard, view) in enumerate(views)
     ]
-    qkv_g, out_g, up_a, up_b, down_a, down_b = gathers
-    small = SmallGather(me, small_tiles, g_send.at[6], g_recv.at[6])
+    qkv_a, qkv_b, out_g, up_a, up_b, down_a, down_b = gathers
+    small = SmallGather(me, small_tiles, small_lines, g_send.at[7], g_recv.at[7])
     small.first(gains, biases, up_bias)
     barrier(me)
     small.second()
-    qkv_g.first()
+    qkv_a.first()
     own_rows = pl.ds(pl.multiple_of(me.h * ROWS, ROWS), ROWS)
     hidden_masks(segment[own_rows, :], kinds[own_rows, :], mask)
+    qkv_a.relay(1)
     small.third()
-    qkv_g.relay(1)
-    qkv_g.forward(0)
-    qkv_g.relay(2)
-    qkv_g.forward(1)
-    qkv_g.relay(3)
-    qkv_g.own_across()
+    qkv_a.relay(2)
+    qkv_a.relay(3)
+    qkv_b.first()
+    down_b.first()
     out_g.first()
     up_a.first()
+    qkv_a.own_across()
     small.fourth(gb, upb)
-    qkv_g.forward(2)
-    qkv_g.forward(3)
-    qkv_g.neighbours_across()
-    up_b.first()
-    out_g.second()
     load_tok.wait()
 
     def norm_one(i, carry):
@@ -536,11 +552,15 @@
         return carry
 
     lax.fori_loop(0, T // 256, norm_one, 0)
-    qkv_g.diagonal_across()
-    up_a.second()
+    for n in range(2):
+        qkv_a.other_across(n)
+    for k in (1, 2, 3):
+        qkv_b.relay(k)
+    qkv_a.other_across(2)
+    qkv_b.own_across()
+    up_b.first()
     down_a.first()
-    down_b.first()
-    qkv_g.fifth()
+    qkv_a.fifth()
 
     def at_step(i, steps):
         for n, actions in steps.items():
@@ -550,23 +570,41 @@
                 for action in actions:
                     action()
 
-    def project(i, carry):
-        r = block(i, 512)
+    blocks = T // 512
+
+    def project(i):
+        c, r = i // blocks, block(lax.rem(i, blocks), 512)
         x = normed[r, :]
-        q = (dot(x, w_qkv[0].reshape(D, D)) + gb[3:4, :]).astype(bf16) * jnp.asarray(0.125, bf16)
-        k = dot(x, w_qkv[1].reshape(D, D)).astype(bf16)
-        v = (dot(x, w_qkv[2].reshape(D, D)) + gb[4:5, :]).astype(bf16)
-        for p in range(4):
-            for s, value in enumerate((q, k, v)):
-                packed[s, p, r, :] = value[:, LANES * p : LANES * p + LANES]
-        at_step(i, {1: [up_b.second], 2: [out_g.third]})
-        return carry
-
-    lax.fori_loop(0, T // 512, project, 0)
+        values = []
+        for s in range(3):
+            value = dot(x, w_qkv[c, s].reshape(D, 256))
+            if s != 1:
+                row = 3 + s // 2
+                value = value + jnp.concatenate(
+                    [gb[row : row + 1, columns(c, LANES)], gb[row : row + 1, columns(2 + c, LANES)]], axis=1
+                )
+            value = value.astype(bf16)
+            values.append(value * jnp.asarray(0.125, bf16) if s == 0 else value)
+        return values
+
+    def keep(i, projected):
+        c, r = i // blocks, block(lax.rem(i, blocks), 512)
+        for n in range(2):
+            for s, value in enumerate(projected):
+                packed[s, 2 * n + c, r, :] = value[:, LANES * n : LANES * n + LANES]
+
+    start = me.z * 0
+    keep(start, project(start))
 
     def attend(i, carry):
-        items = [(4 * i + u, p) for u in range(4) for p in range(4)]
-        scores = [dot(two_heads(packed[1, p, block(r, SEQ), :]), packed[0, p, block(r, SEQ), :], NT) for r, p in items]
+        c, b = i // blocks, lax.rem(i, blocks)
+        items = [(4 * b + u, 2 * n + c) for u in range(4) for n in range(2)]
+        scores = [
+            dot(two_heads(packed[1, p, block(r, SEQ), :]), packed[0, p, block(r, SEQ), :], NT) for r, p in items
+        ]
+        values = [two_heads(packed[2, p, block(r, SEQ), :]) for r, p in items]
+        following = jnp.minimum(i + 1, 2 * blocks - 1)
+        projected = project(following)
         weights = []
         for (r, p), pair in zip(items, scores):
             heads = []
@@ -577,12 +615,24 @@
                 att[r, 2 * p + h] = a
                 heads.append(a)
             weights.append(jnp.concatenate(heads, axis=0))
-        for (r, p), pair in zip(items, weights):
-            mix[p, block(r, SEQ), :] = dot(pair, two_heads(packed[2, p, block(r, SEQ), :]), TN).astype(bf16)
-        at_step(i, {0: [up_a.third], 1: [out_g.fourth, down_a.second], 2: [up_b.third], 3: [down_b.second, up_a.fourth]})
+        for (r, p), pair, value in zip(items, weights, values):
+            mix[p, block(r, SEQ), :] = dot(pair, value, TN).astype(bf16)
+        keep(following, projected)
+        at_step(
+            i,
+            {
+                0: [lambda: qkv_b.other_across(0), lambda: qkv_b.other_across(1), out_g.second, up_a.second],
+                1: [lambda: qkv_b.other_across(2)],
+                2: [qkv_b.fifth, up_b.second, down_b.second],
+                3: [out_g.third],
+                5: [up_a.third],
+                6: [out_g.fourth],
+                7: [up_b.third, down_a.second],
+            },
+        )
         return carry
 
-    lax.fori_loop(0, ROWS // 4, attend, 0)
+    lax.fori_loop(0, 2 * blocks, attend, 0)
     out_g.fifth()
 
     def middle_of(r):
@@ -596,26 +646,36 @@
         middle = middle.astype(bf16)
         for p in range(4):
             gmix[p, r, :] = middle[:, LANES * p : LANES * p + LANES]
+        at_step(i, {1: [up_a.fourth]})
         return carry
 
     lax.fori_loop(0, T // 512, norm_two, 0)
     up_b.fourth()
     up_a.fifth()
+
+    half_count = count // 2
+
+    def up_columns(j):
+        return w_up[:, :, :, :, 512 * j : 512 * j + 512].reshape(D, 512)
+
+    def hidden_block(columns_in, steps):
+        def body(i, carry):
+            r = block(i, BM)
+            two = tok[r, :]
+            for j in columns_in:
+                cols = slice(512 * j, 512 * j + 512)
+                hidden, slope = gelu_and_slope(dot(two, up_columns(j)) + upb[:, cols])
+                hid[r, cols] = hidden.astype(bf16)
+                gpre[r, cols] = slope.astype(bf16)
+            at_step(i, steps)
+            return carry
+
+        return body
+
+    lax.fori_loop(0, half_count, hidden_block((0, 1), {3: [down_a.third]}), 0)
     up_b.fifth()
-
-    def hidden_block(i, carry):
-        r = block(i, BM)
-        two = tok[r, :]
-        for j in range(4):
-            cols = slice(512 * j, 512 * j + 512)
-            u = dot(two, w_up[:, :, :, :, cols].reshape(D, 512)) + upb[:, cols]
-            hidden, slope = gelu_and_slope(u)
-            hid[r, cols] = hidden.astype(bf16)
-            gpre[r, cols] = slope.astype(bf16)
-        at_step(i, {1: [down_a.third], 3: [down_b.third], 5: [down_a.fourth], 7: [down_b.fourth]})
-        return carry
-
-    lax.fori_loop(0, count, hidden_block, 0)
+    lax.fori_loop(0, half_count, hidden_block((2, 3), {3: [down_a.fourth]}), 0)
+    down_b.third()
     load_cot.wait()
     down_a.fifth()
     down_b.fifth()
@@ -623,17 +683,7 @@
     acc_up[...] = jnp.zeros_like(acc_up)
     acc_q[...] = jnp.zeros_like(acc_q)
 
-    def hidden_back(i, carry):
-        r = block(i, BM)
-        c = cot[r, :]
-        e = jnp.zeros((BM, D), f32)
-        for j in range(4):
-            cols = slice(512 * j, 512 * j + 512)
-            grad_pre = dot(c, w_down[j].reshape(512, D), NT) * gpre[r, cols].astype(f32)
-            acc_up[:, cols] += column_sums(grad_pre)
-            grad_pre = grad_pre.astype(bf16)
-            gpre[r, cols] = grad_pre
-            e = e + dot(grad_pre, w_up[:, :, :, :, cols].reshape(D, 512), NT)
+    def branch_back(r, e, c):
         xhat, rstd = normalized(tiles(gmix, r).astype(f32))
         cot_f32 = c.astype(f32)
         branch = (cot_f32 + norm_back(e, xhat, rstd, gb[1:2, :])).astype(bf16)
@@ -645,9 +695,29 @@
         acc[6] += column_sums(e)
         acc[5] += column_sums(branch.astype(f32))
         acc[7] += column_sums(cot_f32)
+
+    def hidden_back(i, carry):
+        ra, rb = block(i, BM), block(i + half_count, BM)
+        ca, cb, two = cot[ra, :], cot[rb, :], tok[rb, :]
+        ea = eb = 0.0
+        for j in range(4):
+            cols = slice(512 * j, 512 * j + 512)
+            w_up_j, w_down_j = up_columns(j), w_down[j].reshape(512, D)
+            hidden, slope = gelu_and_slope(dot(two, w_up_j) + upb[:, cols])
+            hid[rb, cols] = hidden.astype(bf16)
+            pre_a = dot(ca, w_down_j, NT) * gpre[ra, cols].astype(f32)
+            pre_b = dot(cb, w_down_j, NT) * slope
+            acc_up[:, cols] += column_sums(pre_a) + column_sums(pre_b)
+            pre_a, pre_b = pre_a.astype(bf16), pre_b.astype(bf16)
+            gpre[ra, cols] = pre_a
+            gpre[rb, cols] = pre_b
+            ea = ea + dot(pre_a, w_up_j, NT)
+            eb = eb + dot(pre_b, w_up_j, NT)
+        branch_back(ra, ea, ca)
+        branch_back(rb, eb, cb)
         return carry
 
-    lax.fori_loop(0, count, hidden_back, 0)
+    lax.fori_loop(0, half_count, hidden_back, 0)
 
     units = [
         Scatter(me, *refs, s_send.at[i], s_recv.at[i])
@@ -664,18 +734,17 @@
     ]
     d0, d1, u0, u1, out_u, qkv_u = units
 
-    def grad_down_chunk(half, part):
-        def body(z, carry):
-            o = dot(cot[:, 256 * half : 256 * half + 256], hid[:, block(z, 512)], TN).astype(bf16).T
+    def grad_down_chunk(z, carry):
+        o = dot(cot[...], hid[:, block(z, 512)], TN).astype(bf16).T
+        for half, part in enumerate((p_down0, p_down1)):
             for p in range(GRID_P):
                 for h in range(2):
                     for j in range(2):
                         part[h, z, p, 64 * j : 64 * j + 64] = o[
-                            64 * (2 * p + h) : 64 * (2 * p + h) + 64, LANES * j : LANES * j + LANES
+                            64 * (2 * p + h) : 64 * (2 * p + h) + 64,
+                            256 * half + LANES * j : 256 * half + LANES * j + LANES,
                         ]
-            return carry
-
-        return body
+        return carry
 
     def grad_up_chunk(half, part):
         def body(c, carry):
@@ -692,21 +761,6 @@
 
         return body
 
-    lax.fori_loop(0, 4, grad_down_chunk(0, p_down0), 0)
-    d0.first()
-    lax.fori_loop(0, 4, grad_down_chunk(1, p_down1), 0)
-    d1.first()
-    d0.second()
-    lax.fori_loop(0, 2, grad_up_chunk(0, p_up0), 0)
-    u0.first()
-    d1.second()
-    lax.fori_loop(0, 2, grad_up_chunk(1, p_up1), 0)
-    u1.first()
-    load_tok = pltpu.make_async_copy(tokens_hbm, tok, io_sem.at[0])
-    load_tok.start()
-    u0.second()
-    d0.third()
-
     o = dot(gbr[...], jnp.concatenate([mix[p] for p in range(4)], axis=1), TN).astype(bf16)
     for z in range(GRID_Z):
         for p in range(GRID_P):
@@ -717,6 +771,22 @@
                         32 * d : 32 * d + 32, 256 * h + LANES * j : 256 * h + LANES * j + LANES
                     ]
     out_u.first()
+    lax.fori_loop(0, 4, grad_down_chunk, 0)
+    out_u.second()
+    d0.first()
+    d1.first()
+    lax.fori_loop(0, 2, grad_up_chunk(0, p_up0), 0)
+    d0.second()
+    u0.first()
+    d1.second()
+    lax.fori_loop(0, 2, grad_up_chunk(1, p_up1), 0)
+    u1.first()
+    out_u.third()
+    load_tok = pltpu.make_async_copy(tokens_hbm, tok, io_sem.at[0])
+    load_tok.start()
+    u0.second()
+    d0.third()
+
     u1.second()
     d1.third()
 
@@ -740,18 +810,23 @@
                         for h in range(2)
                     ]
                 )
-            for (r, p), pair in zip(items, slopes):
+            results, sums = [], [0.0] * 4
+            for n, ((r, p), pair) in enumerate(zip(items, slopes)):
                 rows = block(r, SEQ)
                 queries, keys = two_heads(packed[0, p, rows, :]), two_heads(packed[1, p, rows, :])
                 g_q = dot(jnp.concatenate(pair, axis=0), keys, TN) * 0.125
                 g_k = dot(jnp.concatenate(pair, axis=1), queries)
                 weights = jnp.concatenate([att[r, 2 * p], att[r, 2 * p + 1]], axis=1)
                 g_v = dot(weights, two_heads(gmix[p, rows, :]))
-                packed[0, p, rows, :] = g_q.astype(bf16)
-                packed[1, p, rows, :] = g_k.astype(bf16)
-                packed[2, p, rows, :] = g_v.astype(bf16)
-                acc_q[0, p] += column_sums(g_q)
-                acc_q[1, p] += column_sums(g_v)
+                sums[n % 2] = sums[n % 2] + column_sums(g_q)
+                sums[2 + n % 2] = sums[2 + n % 2] + column_sums(g_v)
+                results.append((g_q.astype(bf16), g_k.astype(bf16), g_v.astype(bf16)))
+            for (r, p), result in zip(items, results):
+                for n in range(3):
+                    packed[n, p, block(r, SEQ), :] = result[n]
+            for pp in range(2):
+                acc_q[0, 2 * half + pp] += sums[pp]
+                acc_q[1, 2 * half + pp] += sums[2 + pp]
             at_step(i, steps)
             return carry
 
@@ -772,42 +847,43 @@
 
         return body
 
-    lax.fori_loop(0, ROWS // 4, attend_back(me.sib, {0: [u0.third], 1: [d0.fourth], 3: [out_u.second]}), 0)
+    lax.fori_loop(0, ROWS // 4, attend_back(me.sib, {1: [out_u.fourth], 2: [u0.third]}), 0)
     lax.fori_loop(0, 3, grad_qkv_half(me.sib), 0)
     qkv_u.first()
+    d0.fourth()
     u1.third()
-    d1.fourth()
-    lax.fori_loop(0, ROWS // 4, attend_back(me.h, {1: [out_u.third], 2: [u0.fourth]}), 0)
+    lax.fori_loop(0, ROWS // 4, attend_back(me.h, {3: [d1.fourth]}), 0)
     lax.fori_loop(0, 3, grad_qkv_half(me.h), 0)
     qkv_u.second()
-    u1.fourth()
-    out_u.fourth()
+    u0.fourth()
     load_tok.wait()
 
     def grad_copy(i):
         return pltpu.make_async_copy(
-            grad_stage.at[parity(i)], grad_hbm.at[block(i, BM), :], out_sem.at[2 + parity(i)]
+            grad_stage.at[parity(i)], grad_hbm.at[block(i, BACK), :], out_sem.at[parity(i)]
         )
 
     def norm_one_back(i, carry):
-        r = block(i, BM)
+        r = block(i, BACK)
 
         @pl.when(i >= 2)
         def _():
             grad_copy(i - 2).wait()
 
-        e = dot(tiles(packed.at[0], r), w_qkv[0].reshape(D, D), NT)
-        e = e + dot(tiles(packed.at[1], r), w_qkv[1].reshape(D, D), NT)
-        e = e + dot(tiles(packed.at[2], r), w_qkv[2].reshape(D, D), NT)
+        e = 0.0
+        for c in range(2):
+            for s in range(3):
+                pair = jnp.concatenate([packed[s, c, r, :], packed[s, 2 + c, r, :]], axis=1)
+                e = e + dot(pair, w_qkv[c, s].reshape(D, 256), NT)
         xhat, rstd = normalized(tok[r, :].astype(f32))
         grad_stage[parity(i)] = gbr[r, :].astype(f32) + norm_back(e, xhat, rstd, gb[0:1, :])
         grad_copy(i).start()
         acc[0] += column_sums(e * xhat)
         acc[2] += column_sums(e)
-        at_step(i, {5: [qkv_u.third]})
+        at_step(i, {3: [u1.fourth], 6: [qkv_u.third]})
         return carry
 
-    lax.fori_loop(0, count, norm_one_back, 0)
+    lax.fori_loop(0, back_count, norm_one_back, 0)
     for p in range(4):
         acc[3, :, LANES * p : LANES * p + LANES] = acc_q[0, p]
         acc[4, :, LANES * p : LANES * p + LANES] = acc_q[1, p]
@@ -822,80 +898,86 @@
     small_sum = SmallScatter(me, p_small, small_line, small_sets, s_send.at[6], s_recv.at[6])
     small_sum.first()
 
-    def out_copy(i):
-        return pltpu.make_async_copy(
-            out_stage.at[parity(i)], output_hbm.at[block(i, BM), :], out_sem.at[parity(i)]
-        )
+    def out_copies(i):
+        r = block(i, 512)
+        return [
+            pltpu.make_async_copy(
+                gmix.at[p, r], output_hbm.at[r, pl.ds(LANES * p, LANES)], out_sem.at[2]
+            )
+            for p in range(4)
+        ]
 
     def output_block(i, carry):
-        r = block(i, BM)
-
-        @pl.when(i >= 2)
-        def _():
-            out_copy(i - 2).wait()
-
+        r = block(i, 512)
         total = middle_of(r) + dot(hid[r, :], w_down[...].reshape(2048, D)) + gb[7:8, :]
-        out_stage[parity(i)] = total.astype(bf16)
-        out_copy(i).start()
-        at_step(i, {3: [small_sum.second, qkv_u.fourth]})
+        total = total.astype(bf16)
+        for p in range(4):
+            gmix[p, r, :] = total[:, LANES * p : LANES * p + LANES]
+        for copy in out_copies(i):
+            copy.start()
+        at_step(i, {2: [small_sum.second], 3: [qkv_u.fourth]})
         return carry
 
-    lax.fori_loop(0, count, output_block, 0)
-    for unit, j0 in ((d0, 0), (d1, 2)):
+    lax.fori_loop(0, T // 512, output_block, 0)
+    for unit, rows in ((out_u, OUT_ROWS), (d0, DOWN_ROWS), (d1, DOWN_ROWS + 128), (u0, UP_ROWS), (u1, UP_ROWS + 128)):
         total = unit.fifth()
-        for j in range(2):
-            g_down[:, LANES * (j0 + j) : LANES * (j0 + j) + LANES] = total[64 * j : 64 * j + 64]
-    for unit, j0 in ((u0, 0), (u1, 8)):
-        total = unit.fifth()
-        for j in range(8):
-            g_up[:, LANES * (j0 + j) : LANES * (j0 + j) + LANES] = total[16 * j : 16 * j + 16]
-    total = out_u.fifth()
-    for j in range(2):
-        g_out[:, LANES * j : LANES * j + LANES] = total[32 * j : 32 * j + 32]
-    small_sum.third(g_gains, g_biases, g_up_bias)
-    total = qkv_u.fifth()
-    for s in range(3):
-        for j in range(2):
-            g_qkv[s, :, LANES * j : LANES * j + LANES] = total[64 * s + 32 * j : 64 * s + 32 * j + 32]
-    for i in (count - 2, count - 1):
-        out_copy(i).wait()
+        sums[rows : rows + total.shape[0]] = total
+    small_sum.third(sums)
+    sums[QKV_ROWS : QKV_ROWS + 192] = qkv_u.fifth()
+    for i in range(T // 512):
+        for copy in out_copies(i):
+            copy.wait()
+    for i in (back_count - 2, back_count - 1):
         grad_copy(i).wait()
     for item in gathers + units + [small, small_sum]:
         item.close()
 
 
-def finish_kernel(*refs):
-    for source, target in zip(refs[:9], refs[9:]):
-        target[...] = source[...]
-
-
-def finish(*arrays):
-    steps = 4
-
-    def spec(array, n):
-        if n < 2:
-            return pl.BlockSpec((array.shape[0] // steps, array.shape[1]), lambda i: (i, 0))
-        return pl.BlockSpec(array.shape, lambda i: (0,) * array.ndim)
-
-    specs = [spec(a, n) for n, a in enumerate(arrays)]
-    return pl.pallas_call(
-        finish_kernel,
-        out_shape=tuple(jax.ShapeDtypeStruct(a.shape, a.dtype) for a in arrays),
-        grid=(steps,),
-        in_specs=specs,
-        out_specs=specs,
-        compiler_params=pltpu.CompilerParams(vmem_limit_bytes=VMEM_LIMIT),
-        name="finish",
-    )(*arrays)
-
-
-def layer(tokens, cotangent, qkv, out, up, down, gains, biases, up_bias, segment, kinds):
+def finish_kernel(output, grad, sums_hbm, *refs):
+    targets, stages, sums, sems = refs[:9], refs[9:18], refs[18], refs[19]
+    loads, stores = [], []
+    load_sums = pltpu.make_async_copy(sums_hbm, sums, sems.at[0, 0, 4])
+    load_sums.start()
+    for n in range(4):
+        for a, source in ((1, grad), (0, output)):
+            size = source.shape[0] // 4
+            rows = pl.ds(n * size, size)
+            loads.append(pltpu.make_async_copy(source.at[rows], stages[a].at[rows], sems.at[0, a, n]))
+            stores.append(pltpu.make_async_copy(stages[a].at[rows], targets[a].at[rows], sems.at[1, a, n]))
+    for load in loads:
+        load.start()
+    g_qkv, g_out, g_up, g_down, g_gains, g_biases, g_up_bias = stages[2:]
+    load_sums.wait()
+
+    def tile(start, rows, j):
+        return sums[start + rows * j : start + rows * (j + 1)]
+
+    for j in range(4):
+        g_down[:, LANES * j : LANES * j + LANES] = tile(DOWN_ROWS, 64, j)
+    for j in range(16):
+        g_up[:, LANES * j : LANES * j + LANES] = tile(UP_ROWS, 16, j)
+    for j in range(2):
+        g_out[:, LANES * j : LANES * j + LANES] = tile(OUT_ROWS, 32, j)
+        for s in range(3):
+            g_qkv[s, :, LANES * j : LANES * j + LANES] = tile(QKV_ROWS + 64 * s, 32, j)
+    g_gains[...] = sums[SMALL_ROWS : SMALL_ROWS + 2, 0:16]
+    g_biases[...] = sums[SMALL_ROWS + 2 : SMALL_ROWS + 8, 0:16]
+    g_up_bias[...] = sums[SMALL_ROWS + 8 : SMALL_ROWS + 9, 0:64]
+    for n in range(2, 9):
+        stores.append(pltpu.make_async_copy(stages[n], targets[n], sems.at[2, n // 5, n % 5]))
+        stores[-1].start()
+    for load, store in zip(loads, stores):
+        load.wait()
+        store.start()
+    for store in stores:
+        store.wait()
+
+
+def finish(output, grad, sums):
     shape = jax.ShapeDtypeStruct
-    T = tokens.shape[0]
-    rows = T // SEQ
     outs = (
-        shape((T, D), bf16),
-        shape((T, D), f32),
+        shape(output.shape, bf16),
+        shape(grad.shape, f32),
         shape((3, 32, 256), f32),
         shape((32, 256), f32),
         shape((16, 2048), f32),
@@ -904,32 +986,48 @@
         shape((6, 16), f32),
         shape((1, 64), f32),
     )
+    return pl.pallas_call(
+        finish_kernel,
+        out_shape=outs,
+        in_specs=[ANY] * 3,
+        out_specs=[ANY] * 9,
+        scratch_shapes=[pltpu.VMEM(o.shape, o.dtype) for o in outs]
+        + [pltpu.VMEM(sums.shape, f32), pltpu.SemaphoreType.DMA((3, 2, 5))],
+        compiler_params=pltpu.CompilerParams(vmem_limit_bytes=VMEM_LIMIT),
+        name="finish",
+    )(output, grad, sums)
+
+
+def layer(tokens, cotangent, qkv, out, up, down, gains, biases, up_bias, segment, kinds):
+    shape = jax.ShapeDtypeStruct
+    T = tokens.shape[0]
+    rows = T // SEQ
+    outs = (shape((T, D), bf16), shape((T, D), f32), shape((ALL_ROWS, LANES), f32))
     sizes = [128, 128, 128, 128, 64, 192]
-    BM = 256
     V, S = pltpu.VMEM, pltpu.SemaphoreType.DMA
     scratch = [
         V((T, D), bf16), V((T, D), bf16),
-        V((3, 4, 4, 32, 512), bf16), V((4, 4, 32, 512), bf16),
+        V((2, 3, 4, 4, 32, 256), bf16), V((4, 4, 32, 512), bf16),
         V((4, 4, 2, 16, 2048), bf16), V((4, 4, 2, 64, 512), bf16),
         V((8, 512), f32), V((1, 2048), f32), V((rows, SEQ, SEQ), bf16),
         V((T, D), bf16), V((3, 4, T, LANES), bf16), V((rows, 8, SEQ, SEQ), bf16),
         V((4, T, LANES), bf16), V((T, 2048), bf16), V((T, 2048), bf16),
         V((T, D), bf16), V((4, T, LANES), bf16), V((8, 8, 512), f32), V((8, 2048), f32),
         V((2, 4, 8, LANES), f32),
-        V((2, BM, D), bf16), V((2, BM, D), f32),
+        V((2, 256, D), f32),
     ]
     scratch += [V((2, 4, 4, r, LANES), bf16) for r in sizes] + [V((4, 16, LANES), f32)]
     scratch += [V((4, 4, r, LANES), bf16) for r in sizes]
     scratch += [V((2, 2, r, LANES), bf16) for r in sizes]
     scratch += [V((2, 4, r, LANES), bf16) for r in sizes]
     scratch += [V((3, r, LANES), bf16) for r in sizes]
-    scratch += [V((4, 2, 4, 16, LANES), bf16), V((3, 16, LANES), f32), V((8, 16, LANES), f32)]
-    scratch += [S((7, 19)), S((7, 19)), S((6,)), S((7, 10)), S((7, 10)), S((2,)), S((4,))]
+    scratch += [V((4, 2, 16, LANES), bf16), V((4, 16, LANES), bf16), V((3, 16, LANES), f32), V((8, 16, LANES), f32)]
+    scratch += [S((8, 19)), S((8, 19)), S((7,)), S((7, 10)), S((7, 10)), S((2,)), S((3,))]
     return pl.pallas_call(
         layer_kernel,
         out_shape=outs,
         in_specs=[ANY] * 6 + [VM] * 5,
-        out_specs=[ANY] * 2 + [VM] * 7,
+        out_specs=[ANY] * 2 + [VM],
         scratch_shapes=scratch,
         compiler_params=pltpu.CompilerParams(
             collective_id=0, has_side_effects=True, vmem_limit_bytes=VMEM_LIMIT

time: 126 us -> 118 us (0.937)
  Pallas kernels: 125 us -> 117 us
    pallas_call x1, Pallas kernels: 119 us -> 111 us  [layer(): pl.pallas_call(layer_kernel, out_shape=outs, in_specs=[ANY] * 6 + [VM] *...]
where the time goes in v3:
time: 118 us
  Pallas kernels  117 us (99%)
    pallas_call x1, Pallas kernels, layer(): pl.pallas_call(layer_kernel, out_shape=outs, in_specs=[ANY] * 6 + [VM] *...  111 us
    pallas_call x1, Pallas kernels, finish(): pl.pallas_call(finish_kernel, out_shape=outs, in_specs=[ANY] * 3, out_spe...  5.87 us

profile of v3, /device:TPU:0, one launch (start us, length us, event | category | flops | bytes accessed | tf_op | source)
XLA Modules:
  0.0 117.9 jit_solution(17891689301399436488)
XLA Ops:
  0.6 111.2 %layer.1 = (bf16[2048,512]{1,0:T(8,128)(2,1)}, f32[2048,512]{1,0:T(8,128)}, f32[784,128]{1,0:T(8,128)}) custom-call(bf16[2048,512]{1,0:T(8,128)(2,1)} %tokens_hbm.1, bf16[2048,512]{1,0:T(8,128)(2,1)} %cot_hbm.1, bf16[3,32,256]{2,1,0:T(8,128)(2,1)} %qkv_s.1, bf16[32,256]{1,0:T(8,128)(2,1)} %out_s.1, bf16[16,2048]{1,0:T(8,128)(2,1)} %up_s.1, ...), custom_call_target="tpu_custom_call" | custom-call | tf_op jit(solution)/shard_map/layer/pallas_call | solution.py:1026
  111.8 5.9 %finish.1 = (bf16[2048,512]{1,0:T(8,128)(2,1)}, f32[2048,512]{1,0:T(8,128)}, f32[3,32,256]{2,1,0:T(8,128)}, f32[32,256]{1,0:T(8,128)}, f32[16,2048]{1,0:T(8,128)...) custom-call(bf16[2048,512]{1,0:T(8,128)(2,1)} %get-tuple-element.21.output, ...), custom_call_target="tpu_custom_call" | custom-call | tf_op jit(solution)/shard_map/finish/pallas_call | solution.py:989

commit v4 on v3

--- a/solution.py
+++ b/solution.py
@@ -728,11 +728,11 @@
                 (p_up0, core2, cross2, sets2, line2),
                 (p_up1, core3, cross3, sets3, line3),
                 (p_out, core4, cross4, sets4, line4),
-                (p_qkv, core5, cross5, sets5, line5),
+                *((p_qkv.at[n], core5.at[n], cross5.at[n], sets5.at[n], line5.at[n]) for n in range(3)),
             )
         )
     ]
-    d0, d1, u0, u1, out_u, qkv_u = units
+    d0, d1, u0, u1, out_u, *qkv_u = units
 
     def grad_down_chunk(z, carry):
         o = dot(cot[...], hid[:, block(z, 512)], TN).astype(bf16).T
@@ -832,7 +832,7 @@
 
         return body
 
-    def grad_qkv_half(half):
+    def grad_qkv_half(half, steps):
         def body(s, carry):
             wide = jnp.concatenate([packed[s, 2 * half], packed[s, 2 * half + 1]], axis=1)
             o = dot(normed[...], wide, TN).astype(bf16)
@@ -840,21 +840,20 @@
                 for p in range(GRID_P):
                     d = z * 4 + p
                     for j in range(2):
-                        p_qkv[half, z, p, pl.ds(pl.multiple_of(64 * s + 32 * j, 32), 32)] = o[
+                        p_qkv[s, half, z, p, 32 * j : 32 * j + 32] = o[
                             32 * d : 32 * d + 32, LANES * j : LANES * j + LANES
                         ]
+            at_step(s, steps)
             return carry
 
         return body
 
     lax.fori_loop(0, ROWS // 4, attend_back(me.sib, {1: [out_u.fourth], 2: [u0.third]}), 0)
-    lax.fori_loop(0, 3, grad_qkv_half(me.sib), 0)
-    qkv_u.first()
+    lax.fori_loop(0, 3, grad_qkv_half(me.sib, {n: [qkv_u[n].first] for n in range(3)}), 0)
     d0.fourth()
     u1.third()
     lax.fori_loop(0, ROWS // 4, attend_back(me.h, {3: [d1.fourth]}), 0)
-    lax.fori_loop(0, 3, grad_qkv_half(me.h), 0)
-    qkv_u.second()
+    lax.fori_loop(0, 3, grad_qkv_half(me.h, {n: [qkv_u[n].second] for n in range(3)}), 0)
     u0.fourth()
     load_tok.wait()
 
@@ -876,11 +875,12 @@
                 pair = jnp.concatenate([packed[s, c, r, :], packed[s, 2 + c, r, :]], axis=1)
                 e = e + dot(pair, w_qkv[c, s].reshape(D, 256), NT)
         xhat, rstd = normalized(tok[r, :].astype(f32))
-        grad_stage[parity(i)] = gbr[r, :].astype(f32) + norm_back(e, xhat, rstd, gb[0:1, :])
+        grad = gbr[r, :].astype(f32) + norm_back(e, xhat, rstd, gb[0:1, :])
+        grad_stage[parity(i)] = grad.astype(bf16)
         grad_copy(i).start()
         acc[0] += column_sums(e * xhat)
         acc[2] += column_sums(e)
-        at_step(i, {3: [u1.fourth], 6: [qkv_u.third]})
+        at_step(i, {0: [qkv_u[0].third], 1: [u1.fourth], 2: [qkv_u[1].third, qkv_u[2].third]})
         return carry
 
     lax.fori_loop(0, back_count, norm_one_back, 0)
@@ -895,7 +895,7 @@
         ]
         rows += [jnp.zeros((4, LANES), f32)]
         p_small[z] = jnp.concatenate(rows, axis=0)
-    small_sum = SmallScatter(me, p_small, small_line, small_sets, s_send.at[6], s_recv.at[6])
+    small_sum = SmallScatter(me, p_small, small_line, small_sets, s_send.at[8], s_recv.at[8])
     small_sum.first()
 
     def out_copies(i):
@@ -915,7 +915,7 @@
             gmix[p, r, :] = total[:, LANES * p : LANES * p + LANES]
         for copy in out_copies(i):
             copy.start()
-        at_step(i, {2: [small_sum.second], 3: [qkv_u.fourth]})
+        at_step(i, {0: [qkv_u[0].fourth], 1: [small_sum.second, qkv_u[1].fourth], 2: [qkv_u[2].fourth]})
         return carry
 
     lax.fori_loop(0, T // 512, output_block, 0)
@@ -923,7 +923,8 @@
         total = unit.fifth()
         sums[rows : rows + total.shape[0]] = total
     small_sum.third(sums)
-    sums[QKV_ROWS : QKV_ROWS + 192] = qkv_u.fifth()
+    for n in range(3):
+        sums[QKV_ROWS + 64 * n : QKV_ROWS + 64 * n + 64] = qkv_u[n].fifth()
     for i in range(T // 512):
         for copy in out_copies(i):
             copy.wait()
@@ -934,7 +935,8 @@
 
 
 def finish_kernel(output, grad, sums_hbm, *refs):
-    targets, stages, sums, sems = refs[:9], refs[9:18], refs[18], refs[19]
+    targets, stages, sums, grad_in, sems = refs[:9], refs[9:18], refs[18], refs[19], refs[20]
+    staged = (stages[0], grad_in)
     loads, stores = [], []
     load_sums = pltpu.make_async_copy(sums_hbm, sums, sems.at[0, 0, 4])
     load_sums.start()
@@ -942,7 +944,7 @@
         for a, source in ((1, grad), (0, output)):
             size = source.shape[0] // 4
             rows = pl.ds(n * size, size)
-            loads.append(pltpu.make_async_copy(source.at[rows], stages[a].at[rows], sems.at[0, a, n]))
+            loads.append(pltpu.make_async_copy(source.at[rows], staged[a].at[rows], sems.at[0, a, n]))
             stores.append(pltpu.make_async_copy(stages[a].at[rows], targets[a].at[rows], sems.at[1, a, n]))
     for load in loads:
         load.start()
@@ -966,8 +968,11 @@
     for n in range(2, 9):
         stores.append(pltpu.make_async_copy(stages[n], targets[n], sems.at[2, n // 5, n % 5]))
         stores[-1].start()
-    for load, store in zip(loads, stores):
+    for i, (load, store) in enumerate(zip(loads, stores)):
         load.wait()
+        if i % 2 == 0:
+            rows = slice(i // 2 * size, (i // 2 + 1) * size)
+            stages[1][rows] = grad_in[rows].astype(f32)
         store.start()
     for store in stores:
         store.wait()
@@ -992,7 +997,7 @@
         in_specs=[ANY] * 3,
         out_specs=[ANY] * 9,
         scratch_shapes=[pltpu.VMEM(o.shape, o.dtype) for o in outs]
-        + [pltpu.VMEM(sums.shape, f32), pltpu.SemaphoreType.DMA((3, 2, 5))],
+        + [pltpu.VMEM(sums.shape, f32), pltpu.VMEM(grad.shape, bf16), pltpu.SemaphoreType.DMA((3, 2, 5))],
         compiler_params=pltpu.CompilerParams(vmem_limit_bytes=VMEM_LIMIT),
         name="finish",
     )(output, grad, sums)
@@ -1002,8 +1007,8 @@
     shape = jax.ShapeDtypeStruct
     T = tokens.shape[0]
     rows = T // SEQ
-    outs = (shape((T, D), bf16), shape((T, D), f32), shape((ALL_ROWS, LANES), f32))
-    sizes = [128, 128, 128, 128, 64, 192]
+    outs = (shape((T, D), bf16), shape((T, D), bf16), shape((ALL_ROWS, LANES), f32))
+    sizes = [128, 128, 128, 128, 64]
     V, S = pltpu.VMEM, pltpu.SemaphoreType.DMA
     scratch = [
         V((T, D), bf16), V((T, D), bf16),
@@ -1014,15 +1019,15 @@
         V((4, T, LANES), bf16), V((T, 2048), bf16), V((T, 2048), bf16),
         V((T, D), bf16), V((4, T, LANES), bf16), V((8, 8, 512), f32), V((8, 2048), f32),
         V((2, 4, 8, LANES), f32),
-        V((2, 256, D), f32),
+        V((2, 512, D), bf16),
     ]
-    scratch += [V((2, 4, 4, r, LANES), bf16) for r in sizes] + [V((4, 16, LANES), f32)]
-    scratch += [V((4, 4, r, LANES), bf16) for r in sizes]
-    scratch += [V((2, 2, r, LANES), bf16) for r in sizes]
-    scratch += [V((2, 4, r, LANES), bf16) for r in sizes]
-    scratch += [V((3, r, LANES), bf16) for r in sizes]
+    scratch += [V((2, 4, 4, r, LANES), bf16) for r in sizes] + [V((3, 2, 4, 4, 64, LANES), bf16)] + [V((4, 16, LANES), f32)]
+    scratch += [V((4, 4, r, LANES), bf16) for r in sizes] + [V((3, 4, 4, 64, LANES), bf16)]
+    scratch += [V((2, 2, r, LANES), bf16) for r in sizes] + [V((3, 2, 2, 64, LANES), bf16)]
+    scratch += [V((2, 4, r, LANES), bf16) for r in sizes] + [V((3, 2, 4, 64, LANES), bf16)]
+    scratch += [V((3, r, LANES), bf16) for r in sizes] + [V((3, 3, 64, LANES), bf16)]
     scratch += [V((4, 2, 16, LANES), bf16), V((4, 16, LANES), bf16), V((3, 16, LANES), f32), V((8, 16, LANES), f32)]
-    scratch += [S((8, 19)), S((8, 19)), S((7,)), S((7, 10)), S((7, 10)), S((2,)), S((3,))]
+    scratch += [S((8, 19)), S((8, 19)), S((7,)), S((9, 10)), S((9, 10)), S((2,)), S((3,))]
     return pl.pallas_call(
         layer_kernel,
         out_shape=outs,

time: 118 us -> 115 us (0.975)
  Pallas kernels: 117 us -> 114 us
    pallas_call x1, Pallas kernels: 5.87 us -> 4.17 us  [finish(): pl.pallas_call(finish_kernel, out_shape=outs, in_specs=[ANY] * 3, out_spe...]
where the time goes in v4:
time: 115 us
  Pallas kernels  114 us (99%)
    pallas_call x1, Pallas kernels, layer(): pl.pallas_call(layer_kernel, out_shape=outs, in_specs=[ANY] * 6 + [VM] *...  110 us
    pallas_call x1, Pallas kernels, finish(): pl.pallas_call(finish_kernel, out_shape=outs, in_specs=[ANY] * 3, out_spe...  4.17 us

profile of v4, /device:TPU:0, one launch (start us, length us, event | category | flops | bytes accessed | tf_op | source)
XLA Modules:
  0.0 115.0 jit_solution(5970193210637937174)
XLA Ops:
  0.6 110.0 %layer.1 = (bf16[2048,512]{1,0:T(8,128)(2,1)}, bf16[2048,512]{1,0:T(8,128)(2,1)}, f32[784,128]{1,0:T(8,128)}) custom-call(bf16[2048,512]{1,0:T(8,128)(2,1)} %tokens_hbm.1, bf16[2048,512]{1,0:T(8,128)(2,1)} %cot_hbm.1, bf16[3,32,256]{2,1,0:T(8,128)(2,1)} %qkv_s.1, bf16[32,256]{1,0:T(8,128)(2,1)} %out_s.1, bf16[16,2048]{1,0:T(8,128)(2,1)} %up_s.1, ...), custom_call_target="tpu_custom_call" | custom-call | tf_op jit(solution)/shard_map/layer/pallas_call | solution.py:1031
  110.7 4.2 %finish.1 = (bf16[2048,512]{1,0:T(8,128)(2,1)}, f32[2048,512]{1,0:T(8,128)}, f32[3,32,256]{2,1,0:T(8,128)}, f32[32,256]{1,0:T(8,128)}, f32[16,2048]{1,0:T(8,128)...) custom-call(bf16[2048,512]{1,0:T(8,128)(2,1)} %get-tuple-element.21.output, ...), custom_call_target="tpu_custom_call" | custom-call | tf_op jit(solution)/shard_map/finish/pallas_call | solution.py:994

commit v5 on v4

--- a/solution.py
+++ b/solution.py
@@ -880,7 +880,7 @@
         grad_copy(i).start()
         acc[0] += column_sums(e * xhat)
         acc[2] += column_sums(e)
-        at_step(i, {0: [qkv_u[0].third], 1: [u1.fourth], 2: [qkv_u[1].third, qkv_u[2].third]})
+        at_step(i, {0: [qkv_u[0].third], 1: [u1.fourth, qkv_u[1].third], 2: [qkv_u[2].third], 3: [qkv_u[0].fourth]})
         return carry
 
     lax.fori_loop(0, back_count, norm_one_back, 0)
@@ -915,7 +915,7 @@
             gmix[p, r, :] = total[:, LANES * p : LANES * p + LANES]
         for copy in out_copies(i):
             copy.start()
-        at_step(i, {0: [qkv_u[0].fourth], 1: [small_sum.second, qkv_u[1].fourth], 2: [qkv_u[2].fourth]})
+        at_step(i, {0: [qkv_u[1].fourth], 1: [small_sum.second, qkv_u[2].fourth]})
         return carry
 
     lax.fori_loop(0, T // 512, output_block, 0)

time: 115 us -> 115 us (level)
  no operation moved by 1% of the time
where the time goes in v5:
time: 115 us
  Pallas kernels  114 us (99%)
    pallas_call x1, Pallas kernels, layer(): pl.pallas_call(layer_kernel, out_shape=outs, in_specs=[ANY] * 6 + [VM] *...  110 us
    pallas_call x1, Pallas kernels, finish(): pl.pallas_call(finish_kernel, out_shape=outs, in_specs=[ANY] * 3, out_spe...  4.17 us

profile of v5, /device:TPU:0, one launch (start us, length us, event | category | flops | bytes accessed | tf_op | source)
XLA Modules:
  0.0 114.9 jit_solution(13609247571897098415)
XLA Ops:
  0.6 109.9 %layer.1 = (bf16[2048,512]{1,0:T(8,128)(2,1)}, bf16[2048,512]{1,0:T(8,128)(2,1)}, f32[784,128]{1,0:T(8,128)}) custom-call(bf16[2048,512]{1,0:T(8,128)(2,1)} %tokens_hbm.1, bf16[2048,512]{1,0:T(8,128)(2,1)} %cot_hbm.1, bf16[3,32,256]{2,1,0:T(8,128)(2,1)} %qkv_s.1, bf16[32,256]{1,0:T(8,128)(2,1)} %out_s.1, bf16[16,2048]{1,0:T(8,128)(2,1)} %up_s.1, ...), custom_call_target="tpu_custom_call" | custom-call | tf_op jit(solution)/shard_map/layer/pallas_call | solution.py:1031
  110.5 4.2 %finish.1 = (bf16[2048,512]{1,0:T(8,128)(2,1)}, f32[2048,512]{1,0:T(8,128)}, f32[3,32,256]{2,1,0:T(8,128)}, f32[32,256]{1,0:T(8,128)}, f32[16,2048]{1,0:T(8,128)...) custom-call(bf16[2048,512]{1,0:T(8,128)(2,1)} %get-tuple-element.21.output, ...), custom_call_target="tpu_custom_call" | custom-call | tf_op jit(solution)/shard_map/finish/pallas_call | solution.py:994
